TPU v7x, 128 devices: a whole 4x4x4 slice. The times are simulated.
128 devices in a mesh: clip: 8 (over y_hi, z), seq: 16 (over x, y_lo, core).
Axes of the slice: x: 4, y: 4 (y_hi: 2, y_lo: 2; y = y_hi * 2 + y_lo), z: 4, core: 2. Of those that a mesh axis runs over, the one named last changes fastest.
Arguments:
- query_raw: bfloat16 [16384, 4096], P(('clip', 'seq')), may hold values from -400 to 400
- key_raw: bfloat16 [16384, 4096], P(('clip', 'seq')), may hold values from -400 to 400
- values: bfloat16 [16384, 4096], P(('clip', 'seq')), may hold values from -6 to 6
- query_tan: bfloat16 [16384, 4096], P(('clip', 'seq')), may hold values from -2000 to 2000
- key_tan: bfloat16 [16384, 4096], P(('clip', 'seq')), may hold values from -2000 to 2000
- values_tan: bfloat16 [16384, 4096], P(('clip', 'seq')), may hold values from -6 to 6
- query_gain: float32 [4096], P('clip'), may hold values from 0.5 to 2
- key_gain: float32 [4096], P('clip'), may hold values from 0.5 to 2
Outputs:
- attended: bfloat16 [16384, 4096], P(('clip', 'seq'))
- attended_tan: bfloat16 [16384, 4096], P(('clip', 'seq'))
All inputs are finite; a program needn't handle non-finite values.
Results may differ from a plain program's by a relative error of at most 0.0163.
Values may be sent and summed in bfloat16 or wider, within the bound.
A program may use at most 64 MiB of HBM per device.

v0:
```python
import jax
import jax.numpy as jnp
from jax import lax
from jax.sharding import PartitionSpec as P

HEADS = 32
HD = 128


epsilon = 1e-06


def normalize(raw, tangent, gain, square_sum, cross_sum, width):
    rawf = raw.astype(jnp.float32)
    tanf = tangent.astype(jnp.float32)
    root = jnp.sqrt(square_sum / width + epsilon)
    mixed = cross_sum / width
    normed = (gain * rawf / root).astype(jnp.bfloat16)
    normed_tan = (gain * (tanf / root - rawf * mixed / root**3)).astype(jnp.bfloat16)
    return (normed, normed_tan)


def attend(pieces):
    query, keys, vals, query_d, keys_d, vals_d = [
        p.reshape(p.shape[0], p.shape[2], p.shape[3]) for p in pieces
    ]
    length = query.shape[0]
    heads_here = query.shape[1]
    block = min(512, length)
    scale = HD ** (-0.5)

    def one_block(start):
        query_blk = lax.dynamic_slice_in_dim(query, start, block, 0)
        query_d_blk = lax.dynamic_slice_in_dim(query_d, start, block, 0)
        scores = (
            jnp.einsum("qhd,khd->hqk", query_blk, keys, preferred_element_type=jnp.float32) * scale
        )
        top = jnp.max(scores, axis=-1, keepdims=True)
        weights = jnp.exp(scores - top)
        weights = weights / jnp.sum(weights, axis=-1, keepdims=True)
        first = jnp.einsum("qhd,khd->hqk", query_d_blk, keys, preferred_element_type=jnp.float32)
        second = jnp.einsum("qhd,khd->hqk", query_blk, keys_d, preferred_element_type=jnp.float32)
        scores_tan = (first + second) * scale
        weights_tan = weights * (scores_tan - jnp.sum(weights * scores_tan, axis=-1, keepdims=True))
        weights_low = weights.astype(jnp.bfloat16)
        weights_tan_low = weights_tan.astype(jnp.bfloat16)
        out = jnp.einsum(
            "hqk,khd->qhd", weights_low, vals, preferred_element_type=jnp.float32
        ).astype(jnp.bfloat16)
        out_tan = (
            jnp.einsum("hqk,khd->qhd", weights_tan_low, vals, preferred_element_type=jnp.float32)
            + jnp.einsum("hqk,khd->qhd", weights_low, vals_d, preferred_element_type=jnp.float32)
        ).astype(jnp.bfloat16)
        return (out, out_tan)

    starts = jnp.arange(length // block, dtype=jnp.int32) * block
    outs, outs_tan = lax.map(one_block, starts)
    return (outs.reshape(length, 1, heads_here, HD), outs_tan.reshape(length, 1, heads_here, HD))


def on_device(query_raw, key_raw, values, query_tan, key_tan, values_tan, query_gain, key_gain):
    tok_rows, width = query_raw.shape
    groups = lax.axis_size("seq")
    per_group = HEADS // groups
    gain_q, gain_k = (
        lax.all_gather(query_gain, "clip", axis=0, tiled=True),
        lax.all_gather(key_gain, "clip", axis=0, tiled=True),
    )

    def split_heads(array):
        return array.reshape(tok_rows, groups, per_group, HD)

    def local_norm(raw, tangent, gain):
        rawf = raw.astype(jnp.float32)
        tanf = tangent.astype(jnp.float32)
        square_sum = jnp.sum(rawf * rawf, axis=-1, keepdims=True)
        cross_sum = jnp.sum(rawf * tanf, axis=-1, keepdims=True)
        return normalize(raw, tangent, gain, square_sum, cross_sum, width)

    query_norm, query_norm_tan = local_norm(query_raw, query_tan, gain_q)
    key_norm, key_norm_tan = local_norm(key_raw, key_tan, gain_k)
    outs, outs_tan = attend(
        (
            lax.all_to_all(split_heads(query_norm), "seq", split_axis=1, concat_axis=0, tiled=True),
            lax.all_to_all(split_heads(key_norm), "seq", split_axis=1, concat_axis=0, tiled=True),
            lax.all_to_all(split_heads(values), "seq", split_axis=1, concat_axis=0, tiled=True),
            lax.all_to_all(
                split_heads(query_norm_tan), "seq", split_axis=1, concat_axis=0, tiled=True
            ),
            lax.all_to_all(
                split_heads(key_norm_tan), "seq", split_axis=1, concat_axis=0, tiled=True
            ),
            lax.all_to_all(split_heads(values_tan), "seq", split_axis=1, concat_axis=0, tiled=True),
        )
    )
    back, back_tan = (
        lax.all_to_all(outs, "seq", split_axis=0, concat_axis=1, tiled=True),
        lax.all_to_all(outs_tan, "seq", split_axis=0, concat_axis=1, tiled=True),
    )
    return (back.reshape(tok_rows, width), back_tan.reshape(tok_rows, width))


def solution(mesh):
    in_specs = (
        P(("clip", "seq"), None),
        P(("clip", "seq"), None),
        P(("clip", "seq"), None),
        P(("clip", "seq"), None),
        P(("clip", "seq"), None),
        P(("clip", "seq"), None),
        P("clip"),
        P("clip"),
    )
    out_specs = (P(("clip", "seq"), None), P(("clip", "seq"), None))
    return jax.shard_map(
        on_device, mesh=mesh, in_specs=in_specs, out_specs=out_specs, check_vma=False
    )
```

profile of v0, /device:TPU:0, one launch (start us, length us, event | category | flops | bytes accessed | tf_op | source)
XLA Modules:
  0.0 340.9 jit_solution(5383016942199226099)
XLA Ops:
  3.9 31.2 %all-gather.1 = f32[8,1,512]{2,1,0:T(1,128)S(1)} all-gather(f32[1,1,512]{2,1,0:T(1,128)S(1)} %bitcast.111), channel_id=1, replica_groups=mesh['clip'=8,'seq'=16] {'clip'}, dimensions={0}, use_global_device_ids=true | all-gather | bytes 18432 | tf_op jit(solution)/shard_map/all_gather | solution.py:67
  37.6 2.4 copy.50
  40.0 4.7 %all-to-all-start.1 = ((bf16[128,16,2,128]{3,0,2,1:T(8,128)(2,1)}), bf16[128,16,2,128]{3,0,2,1:T(8,128)(2,1)}, u32[]{:S(2)}, u32[]{:S(2)}) async-start(bf16[128,16,2,128]{3,0,2,1:T(8,128)(2,1)} %copy.50), calls=%async_computation.1 | async-start | bytes 2097152 | tf_op jit(solution)/shard_map/all_to_all | solution.py:85
  48.3 30.6 %all-gather = f32[8,1,512]{2,1,0:T(1,128)S(1)} all-gather(f32[1,1,512]{2,1,0:T(1,128)S(1)} %bitcast.112), channel_id=1, replica_groups=mesh['clip'=8,'seq'=16] {'clip'}, dimensions={0}, use_global_device_ids=true | all-gather | bytes 18432 | tf_op jit(solution)/shard_map/all_gather | solution.py:66
  79.6 7.6 %all-to-all-start.4 = ((bf16[128,16,2,128]{3,0,2,1:T(8,128)(2,1)}), bf16[128,16,2,128]{3,0,2,1:T(8,128)(2,1)}, u32[]{:S(2)}, u32[]{:S(2)}) async-start(bf16[128,16,2,128]{3,0,2,1:T(8,128)(2,1)} %copy.59), calls=%async_computation.4 | async-start | bytes 2097152 | tf_op jit(solution)/shard_map/all_to_all | solution.py:90
  89.0 2.3 copy.47
  91.3 12.4 %all-to-all-done.4 = bf16[128,16,2,128]{3,0,2,1:T(8,128)(2,1)} async-done(((bf16[128,16,2,128]{3,0,2,1:T(8,128)(2,1)}), bf16[128,16,2,128]{3,0,2,1:T(8,128)(2,1)}, u32[]{:S(2)}, u32[]{:S(2)}) %all-to-all-start.4) | async-done | bytes 1048608 | tf_op jit(solution)/shard_map/all_to_all | solution.py:90
  103.7 3.7 %all-to-all-start = ((bf16[128,16,2,128]{3,0,2,1:T(8,128)(2,1)}), bf16[128,16,2,128]{3,0,2,1:T(8,128)(2,1)S(1)}, u32[]{:S(2)}, u32[]{:S(2)}) async-start(bf16[128,16,2,128]{3,0,2,1:T(8,128)(2,1)} %copy.47), calls=%async_computation | async-start | bytes 2097152 | tf_op jit(solution)/shard_map/all_to_all | solution.py:84
  108.7 15.1 %all-to-all-done = bf16[128,16,2,128]{3,0,2,1:T(8,128)(2,1)S(1)} async-done(((bf16[128,16,2,128]{3,0,2,1:T(8,128)(2,1)}), bf16[128,16,2,128]{3,0,2,1:T(8,128)(2,1)S(1)}, u32[]{:S(2)}, u32[]{:S(2)}) %all-to-all-start) | async-done | bytes 1048608 | tf_op jit(solution)/shard_map/all_to_all | solution.py:84
  123.8 3.7 %all-to-all-start.3 = ((bf16[128,16,2,128]{3,0,2,1:T(8,128)(2,1)}), bf16[128,16,2,128]{3,0,2,1:T(8,128)(2,1)S(1)}, u32[]{:S(2)}, u32[]{:S(2)}) async-start(bf16[128,16,2,128]{3,0,2,1:T(8,128)(2,1)} %copy.56), calls=%async_computation.3 | async-start | bytes 2097152 | tf_op jit(solution)/shard_map/all_to_all | solution.py:87
  130.4 13.5 %all-to-all-done.3 = bf16[128,16,2,128]{3,0,2,1:T(8,128)(2,1)S(1)} async-done(((bf16[128,16,2,128]{3,0,2,1:T(8,128)(2,1)}), bf16[128,16,2,128]{3,0,2,1:T(8,128)(2,1)S(1)}, u32[]{:S(2)}, u32[]{:S(2)}) %all-to-all-start.3) | async-done | bytes 1048608 | tf_op jit(solution)/shard_map/all_to_all | solution.py:87
  143.9 3.7 %all-to-all-start.2 = ((bf16[128,16,2,128]{3,0,2,1:T(8,128)(2,1)}), bf16[128,16,2,128]{3,0,2,1:T(8,128)(2,1)S(1)}, u32[]{:S(2)}, u32[]{:S(2)}) async-start(bf16[128,16,2,128]{3,0,2,1:T(8,128)(2,1)} %copy.53), calls=%async_computation.2 | async-start | bytes 2097152 | tf_op jit(solution)/shard_map/all_to_all | solution.py:86
  147.6 2.3 copy.61
  149.8 2.3 copy.62
  152.1 11.9 %all-to-all-done.2 = bf16[128,16,2,128]{3,0,2,1:T(8,128)(2,1)S(1)} async-done(((bf16[128,16,2,128]{3,0,2,1:T(8,128)(2,1)}), bf16[128,16,2,128]{3,0,2,1:T(8,128)(2,1)S(1)}, u32[]{:S(2)}, u32[]{:S(2)}) %all-to-all-start.2) | async-done | bytes 1048608 | tf_op jit(solution)/shard_map/all_to_all | solution.py:86
  164.0 4.5 %all-to-all-start.5 = ((bf16[128,16,2,128]{3,0,2,1:T(8,128)(2,1)}), bf16[128,16,2,128]{3,0,2,1:T(8,128)(2,1)}, u32[]{:S(2)}, u32[]{:S(2)}) async-start(bf16[128,16,2,128]{3,0,2,1:T(8,128)(2,1)} %copy.62), calls=%async_computation.5 | async-start | bytes 2097152 | tf_op jit(solution)/shard_map/all_to_all | solution.py:93
  170.0 2.3 copy.60
  174.6 10.2 %all-to-all-done.5 = bf16[128,16,2,128]{3,0,2,1:T(8,128)(2,1)} async-done(((bf16[128,16,2,128]{3,0,2,1:T(8,128)(2,1)}), bf16[128,16,2,128]{3,0,2,1:T(8,128)(2,1)}, u32[]{:S(2)}, u32[]{:S(2)}) %all-to-all-start.5) | async-done | bytes 1048608 | tf_op jit(solution)/shard_map/all_to_all | solution.py:93
  184.8 2.3 copy.63
  187.2 107.6 %while.12 = (s32[]{:T(128)}, bf16[4,512,2,128]{3,1,0,2:T(8,128)(2,1)}, bf16[4,512,2,128]{3,1,0,2:T(8,128)(2,1)}, s32[4]{0:T(128)S(1)}, bf16[2048,2,128]{2,0,1:T(...) while((s32[]{:T(128)}, ...), condition=%wide.region_8.9_spmd, body=%wide.region_4.8_spmd.sunk | while | flops 3255174144 | bytes 126121224 | solution.py:57
  189.7 6.8 %fusion.104 = (f32[2,512]{1,0:T(2,128)S(1)}, f32[2,512,2048]{2,1,0:T(8,128)}) fusion(bf16[2048,2,128]{2,0,1:T(8,128)(2,1)S(1)} %get-tuple-element.201, bf16[2048,2,128]{2,0,1:T(8,128)(2,1)} %get-tuple-element.200, s32[]{:T(128)S(6)} %select_n.5), kind=kOutput, calls=%fused_computation.67.clone.1 | convolution fusion | flops 543164416 | bytes 9703428 | tf_op jit(solution)/shard_map/while/body/eval_jaxpr/sub | solution.py:39
  197.8 2.1 copy-done.9
  199.9 5.5 %multiply_reduce_fusion.3 = (f32[2,512]{1,0:T(2,128)S(1)}, f32[2,512,2048]{2,1,0:T(8,128)}) fusion(f32[2,512,2048]{2,1,0:T(8,128)S(1)} %copy-done.9, f32[2,512]{1,0:T(2,128)S(1)} %get-tuple-element.167, f32[2,512,2048]{2,1,0:T(8,128)S(1)} %fusion.106, bf16[2048,2,128]{2,0,1:T(8,128)(2,1)S(1)} %get-tuple-element.204, ...), kind=kOutput, calls=%fused_computation.2.clone.1 | convolution fusion | flops 547355648 | bytes 26484740 | tf_op jit(solution)/shard_map/while/body/eval_jaxpr/qhd,khd->hqk/dot_general | solution.py:42
  205.4 4.5 %fusion.107 = f32[2,512,128]{2,1,0:T(8,128)S(1)} fusion(bf16[2048,2,128]{2,0,1:T(8,128)(2,1)S(1)} %copy-done.4, f32[2,512,2048]{2,1,0:T(8,128)} %get-tuple-element.168, f32[2,512]{1,0:T(2,128)S(1)} %get-tuple-element.169, f32[2,512,2048]{2,1,0:T(8,128)S(1)} %copy-done.9, f32[2,512]{1,0:T(2,128)S(1)} %get-tuple-element.167), kind=kOutput, calls=%fused_computation.7.clone.1 | convolution fusion | flops 545259520 | bytes 18358272 | tf_op jit(solution)/shard_map/while/body/eval_jaxpr/hqk,khd->qhd/dot_general | solution.py:51
  210.0 2.1 fusion.108
  212.0 2.0 fusion.105
  216.6 6.8 %fusion.104 = (f32[2,512]{1,0:T(2,128)S(1)}, f32[2,512,2048]{2,1,0:T(8,128)}) fusion(bf16[2048,2,128]{2,0,1:T(8,128)(2,1)S(1)} %get-tuple-element.201, bf16[2048,2,128]{2,0,1:T(8,128)(2,1)} %get-tuple-element.200, s32[]{:T(128)S(6)} %select_n.5), kind=kOutput, calls=%fused_computation.67.clone.1 | convolution fusion | flops 543164416 | bytes 9703428 | tf_op jit(solution)/shard_map/while/body/eval_jaxpr/sub | solution.py:39
  224.7 2.1 copy-done.9
  226.8 5.5 %multiply_reduce_fusion.3 = (f32[2,512]{1,0:T(2,128)S(1)}, f32[2,512,2048]{2,1,0:T(8,128)}) fusion(f32[2,512,2048]{2,1,0:T(8,128)S(1)} %copy-done.9, f32[2,512]{1,0:T(2,128)S(1)} %get-tuple-element.167, f32[2,512,2048]{2,1,0:T(8,128)S(1)} %fusion.106, bf16[2048,2,128]{2,0,1:T(8,128)(2,1)S(1)} %get-tuple-element.204, ...), kind=kOutput, calls=%fused_computation.2.clone.1 | convolution fusion | flops 547355648 | bytes 26484740 | tf_op jit(solution)/shard_map/while/body/eval_jaxpr/qhd,khd->hqk/dot_general | solution.py:42
  232.3 4.5 %fusion.107 = f32[2,512,128]{2,1,0:T(8,128)S(1)} fusion(bf16[2048,2,128]{2,0,1:T(8,128)(2,1)S(1)} %copy-done.4, f32[2,512,2048]{2,1,0:T(8,128)} %get-tuple-element.168, f32[2,512]{1,0:T(2,128)S(1)} %get-tuple-element.169, f32[2,512,2048]{2,1,0:T(8,128)S(1)} %copy-done.9, f32[2,512]{1,0:T(2,128)S(1)} %get-tuple-element.167), kind=kOutput, calls=%fused_computation.7.clone.1 | convolution fusion | flops 545259520 | bytes 18358272 | tf_op jit(solution)/shard_map/while/body/eval_jaxpr/hqk,khd->qhd/dot_general | solution.py:51
  236.9 2.1 fusion.108
  238.9 2.0 fusion.105
  243.5 6.8 %fusion.104 = (f32[2,512]{1,0:T(2,128)S(1)}, f32[2,512,2048]{2,1,0:T(8,128)}) fusion(bf16[2048,2,128]{2,0,1:T(8,128)(2,1)S(1)} %get-tuple-element.201, bf16[2048,2,128]{2,0,1:T(8,128)(2,1)} %get-tuple-element.200, s32[]{:T(128)S(6)} %select_n.5), kind=kOutput, calls=%fused_computation.67.clone.1 | convolution fusion | flops 543164416 | bytes 9703428 | tf_op jit(solution)/shard_map/while/body/eval_jaxpr/sub | solution.py:39
  251.6 2.1 copy-done.9
  253.7 5.5 %multiply_reduce_fusion.3 = (f32[2,512]{1,0:T(2,128)S(1)}, f32[2,512,2048]{2,1,0:T(8,128)}) fusion(f32[2,512,2048]{2,1,0:T(8,128)S(1)} %copy-done.9, f32[2,512]{1,0:T(2,128)S(1)} %get-tuple-element.167, f32[2,512,2048]{2,1,0:T(8,128)S(1)} %fusion.106, bf16[2048,2,128]{2,0,1:T(8,128)(2,1)S(1)} %get-tuple-element.204, ...), kind=kOutput, calls=%fused_computation.2.clone.1 | convolution fusion | flops 547355648 | bytes 26484740 | tf_op jit(solution)/shard_map/while/body/eval_jaxpr/qhd,khd->hqk/dot_general | solution.py:42
  259.2 4.5 %fusion.107 = f32[2,512,128]{2,1,0:T(8,128)S(1)} fusion(bf16[2048,2,128]{2,0,1:T(8,128)(2,1)S(1)} %copy-done.4, f32[2,512,2048]{2,1,0:T(8,128)} %get-tuple-element.168, f32[2,512]{1,0:T(2,128)S(1)} %get-tuple-element.169, f32[2,512,2048]{2,1,0:T(8,128)S(1)} %copy-done.9, f32[2,512]{1,0:T(2,128)S(1)} %get-tuple-element.167), kind=kOutput, calls=%fused_computation.7.clone.1 | convolution fusion | flops 545259520 | bytes 18358272 | tf_op jit(solution)/shard_map/while/body/eval_jaxpr/hqk,khd->qhd/dot_general | solution.py:51
  263.8 2.1 fusion.108
  270.4 6.8 %fusion.104 = (f32[2,512]{1,0:T(2,128)S(1)}, f32[2,512,2048]{2,1,0:T(8,128)}) fusion(bf16[2048,2,128]{2,0,1:T(8,128)(2,1)S(1)} %get-tuple-element.201, bf16[2048,2,128]{2,0,1:T(8,128)(2,1)} %get-tuple-element.200, s32[]{:T(128)S(6)} %select_n.5), kind=kOutput, calls=%fused_computation.67.clone.1 | convolution fusion | flops 543164416 | bytes 9703428 | tf_op jit(solution)/shard_map/while/body/eval_jaxpr/sub | solution.py:39
  278.5 2.1 copy-done.9
  280.6 5.5 %multiply_reduce_fusion.3 = (f32[2,512]{1,0:T(2,128)S(1)}, f32[2,512,2048]{2,1,0:T(8,128)}) fusion(f32[2,512,2048]{2,1,0:T(8,128)S(1)} %copy-done.9, f32[2,512]{1,0:T(2,128)S(1)} %get-tuple-element.167, f32[2,512,2048]{2,1,0:T(8,128)S(1)} %fusion.106, bf16[2048,2,128]{2,0,1:T(8,128)(2,1)S(1)} %get-tuple-element.204, ...), kind=kOutput, calls=%fused_computation.2.clone.1 | convolution fusion | flops 547355648 | bytes 26484740 | tf_op jit(solution)/shard_map/while/body/eval_jaxpr/qhd,khd->hqk/dot_general | solution.py:42
  286.1 4.5 %fusion.107 = f32[2,512,128]{2,1,0:T(8,128)S(1)} fusion(bf16[2048,2,128]{2,0,1:T(8,128)(2,1)S(1)} %copy-done.4, f32[2,512,2048]{2,1,0:T(8,128)} %get-tuple-element.168, f32[2,512]{1,0:T(2,128)S(1)} %get-tuple-element.169, f32[2,512,2048]{2,1,0:T(8,128)S(1)} %copy-done.9, f32[2,512]{1,0:T(2,128)S(1)} %get-tuple-element.167), kind=kOutput, calls=%fused_computation.7.clone.1 | convolution fusion | flops 545259520 | bytes 18358272 | tf_op jit(solution)/shard_map/while/body/eval_jaxpr/hqk,khd->qhd/dot_general | solution.py:51
  290.7 2.1 fusion.108
  294.8 3.7 %copy.65 = bf16[2048,1,2,128]{3,2,1,0:T(2,128)(2,1)} copy(bf16[2048,1,2,128]{3,0,2,1:T(8,128)(2,1)} %bitcast.33) | data formatting | bytes 2097152 | tf_op jit(solution)/shard_map/reshape | solution.py:58
  298.5 3.9 %all-to-all-start.6 = ((bf16[2048,1,2,128]{3,2,1,0:T(2,128)(2,1)}), bf16[2048,1,2,128]{3,2,1,0:T(2,128)(2,1)S(1)}, u32[]{:S(2)}, u32[]{:S(2)}) async-start(bf16[2048,1,2,128]{3,2,1,0:T(2,128)(2,1)} %copy.65), calls=%async_computation.6 | async-start | bytes 2097152 | tf_op jit(solution)/shard_map/all_to_all | solution.py:97
  302.4 9.5 %copy.69 = bf16[2048,1,2,128]{3,2,1,0:T(2,128)(2,1)} copy(bf16[2048,1,2,128]{3,0,2,1:T(8,128)(2,1)S(1)} %bitcast.108) | data formatting | bytes 2097152 | tf_op jit(solution)/shard_map/reshape | solution.py:58
  311.9 6.8 %all-to-all-done.6 = bf16[2048,1,2,128]{3,2,1,0:T(2,128)(2,1)S(1)} async-done(((bf16[2048,1,2,128]{3,2,1,0:T(2,128)(2,1)}), bf16[2048,1,2,128]{3,2,1,0:T(2,128)(2,1)S(1)}, u32[]{:S(2)}, u32[]{:S(2)}) %all-to-all-start.6) | async-done | bytes 1048608 | tf_op jit(solution)/shard_map/all_to_all | solution.py:97
  318.6 3.7 %all-to-all-start.7 = ((bf16[2048,1,2,128]{3,2,1,0:T(2,128)(2,1)}), bf16[2048,1,2,128]{3,2,1,0:T(2,128)(2,1)S(1)}, u32[]{:S(2)}, u32[]{:S(2)}) async-start(bf16[2048,1,2,128]{3,2,1,0:T(2,128)(2,1)} %copy.69), calls=%async_computation.7 | async-start | bytes 2097152 | tf_op jit(solution)/shard_map/all_to_all | solution.py:98
  324.4 14.3 %all-to-all-done.7 = bf16[2048,1,2,128]{3,2,1,0:T(2,128)(2,1)S(1)} async-done(((bf16[2048,1,2,128]{3,2,1,0:T(2,128)(2,1)}), bf16[2048,1,2,128]{3,2,1,0:T(2,128)(2,1)S(1)}, u32[]{:S(2)}, u32[]{:S(2)}) %all-to-all-start.7) | async-done | bytes 1048608 | tf_op jit(solution)/shard_map/all_to_all | solution.py:98
  (72 shorter events, 35.7 us)
Async XLA Ops:
  0.6 3.3 copy-start.7
  37.6 8.4 %copy-start.2 = (bf16[128,4096]{1,0:T(8,128)(2,1)S(1)}, bf16[128,4096]{1,0:T(8,128)(2,1)}, u32[]{:S(2)}) copy-start(bf16[128,4096]{1,0:T(8,128)(2,1)} %param.10) | copy-start | bytes 3145732
  40.0 8.3 %copy-start.8 = (f32[512]{0:T(512)S(1)}, f32[512]{0:T(512)}, u32[]{:S(2)}) copy-start(f32[512]{0:T(512)} %param.16) | copy-start | bytes 6148
  40.0 39.6 %all-to-all-start.1 = ((bf16[128,16,2,128]{3,0,2,1:T(8,128)(2,1)}), bf16[128,16,2,128]{3,0,2,1:T(8,128)(2,1)}, u32[]{:S(2)}, u32[]{:S(2)}) async-start(bf16[128,16,2,128]{3,0,2,1:T(8,128)(2,1)} %copy.50), calls=%async_computation.1 | async-start | bytes 2097152 | tf_op jit(solution)/shard_map/all_to_all | solution.py:85
  79.6 24.1 %all-to-all-start.4 = ((bf16[128,16,2,128]{3,0,2,1:T(8,128)(2,1)}), bf16[128,16,2,128]{3,0,2,1:T(8,128)(2,1)}, u32[]{:S(2)}, u32[]{:S(2)}) async-start(bf16[128,16,2,128]{3,0,2,1:T(8,128)(2,1)} %copy.59), calls=%async_computation.4 | async-start | bytes 2097152 | tf_op jit(solution)/shard_map/all_to_all | solution.py:90
  103.7 20.1 %all-to-all-start = ((bf16[128,16,2,128]{3,0,2,1:T(8,128)(2,1)}), bf16[128,16,2,128]{3,0,2,1:T(8,128)(2,1)S(1)}, u32[]{:S(2)}, u32[]{:S(2)}) async-start(bf16[128,16,2,128]{3,0,2,1:T(8,128)(2,1)} %copy.47), calls=%async_computation | async-start | bytes 2097152 | tf_op jit(solution)/shard_map/all_to_all | solution.py:84
  123.8 20.1 %all-to-all-start.3 = ((bf16[128,16,2,128]{3,0,2,1:T(8,128)(2,1)}), bf16[128,16,2,128]{3,0,2,1:T(8,128)(2,1)S(1)}, u32[]{:S(2)}, u32[]{:S(2)}) async-start(bf16[128,16,2,128]{3,0,2,1:T(8,128)(2,1)} %copy.56), calls=%async_computation.3 | async-start | bytes 2097152 | tf_op jit(solution)/shard_map/all_to_all | solution.py:87
  143.9 20.1 %all-to-all-start.2 = ((bf16[128,16,2,128]{3,0,2,1:T(8,128)(2,1)}), bf16[128,16,2,128]{3,0,2,1:T(8,128)(2,1)S(1)}, u32[]{:S(2)}, u32[]{:S(2)}) async-start(bf16[128,16,2,128]{3,0,2,1:T(8,128)(2,1)} %copy.53), calls=%async_computation.2 | async-start | bytes 2097152 | tf_op jit(solution)/shard_map/all_to_all | solution.py:86
  164.0 4.6 %copy-start = (bf16[128,16,2,128]{3,0,2,1:T(8,128)(2,1)}, bf16[128,16,2,128]{3,0,2,1:T(8,128)(2,1)S(1)}, u32[]{:S(2)}) copy-start(bf16[128,16,2,128]{3,0,2,1:T(8,128)(2,1)S(1)} %all-to-all-done.2) | copy-start | bytes 3145732
  164.0 20.8 %all-to-all-start.5 = ((bf16[128,16,2,128]{3,0,2,1:T(8,128)(2,1)}), bf16[128,16,2,128]{3,0,2,1:T(8,128)(2,1)}, u32[]{:S(2)}, u32[]{:S(2)}) async-start(bf16[128,16,2,128]{3,0,2,1:T(8,128)(2,1)} %copy.62), calls=%async_computation.5 | async-start | bytes 2097152 | tf_op jit(solution)/shard_map/all_to_all | solution.py:93
  168.6 5.0 %copy-start.1 = (bf16[128,16,2,128]{3,0,2,1:T(8,128)(2,1)S(1)}, bf16[128,16,2,128]{3,0,2,1:T(8,128)(2,1)}, u32[]{:S(2)}) copy-start(bf16[128,16,2,128]{3,0,2,1:T(8,128)(2,1)} %copy-done) | copy-start | bytes 3145732
  173.6 13.6 %copy-start.3 = (bf16[128,16,2,128]{3,0,1,2:T(8,128)(2,1)S(1)}, bf16[128,16,2,128]{3,0,1,2:T(8,128)(2,1)}, u32[]{:S(2)}) copy-start(bf16[128,16,2,128]{3,0,1,2:T(8,128)(2,1)} %copy.60) | copy-start | bytes 3145732
  196.5 3.4 copy-start.9
  199.9 5.5 %copy-start.4 = (bf16[2048,2,128]{2,0,1:T(8,128)(2,1)S(1)}, bf16[2048,2,128]{2,0,1:T(8,128)(2,1)}, u32[]{:S(2)}) copy-start(bf16[2048,2,128]{2,0,1:T(8,128)(2,1)} %get-tuple-element.202) | copy-start | bytes 3145732 | tf_op jit(solution)/shard_map/while
  205.4 4.6 %copy-start.5 = (bf16[2048,2,128]{2,0,1:T(8,128)(2,1)S(1)}, bf16[2048,2,128]{2,0,1:T(8,128)(2,1)}, u32[]{:S(2)}) copy-start(bf16[2048,2,128]{2,0,1:T(8,128)(2,1)} %get-tuple-element.205) | copy-start | bytes 3145732 | tf_op jit(solution)/shard_map/while
  223.4 3.4 copy-start.9
  226.8 5.5 %copy-start.4 = (bf16[2048,2,128]{2,0,1:T(8,128)(2,1)S(1)}, bf16[2048,2,128]{2,0,1:T(8,128)(2,1)}, u32[]{:S(2)}) copy-start(bf16[2048,2,128]{2,0,1:T(8,128)(2,1)} %get-tuple-element.202) | copy-start | bytes 3145732 | tf_op jit(solution)/shard_map/while
  232.3 4.6 %copy-start.5 = (bf16[2048,2,128]{2,0,1:T(8,128)(2,1)S(1)}, bf16[2048,2,128]{2,0,1:T(8,128)(2,1)}, u32[]{:S(2)}) copy-start(bf16[2048,2,128]{2,0,1:T(8,128)(2,1)} %get-tuple-element.205) | copy-start | bytes 3145732 | tf_op jit(solution)/shard_map/while
  250.3 3.4 copy-start.9
  253.7 5.5 %copy-start.4 = (bf16[2048,2,128]{2,0,1:T(8,128)(2,1)S(1)}, bf16[2048,2,128]{2,0,1:T(8,128)(2,1)}, u32[]{:S(2)}) copy-start(bf16[2048,2,128]{2,0,1:T(8,128)(2,1)} %get-tuple-element.202) | copy-start | bytes 3145732 | tf_op jit(solution)/shard_map/while
  259.2 4.6 %copy-start.5 = (bf16[2048,2,128]{2,0,1:T(8,128)(2,1)S(1)}, bf16[2048,2,128]{2,0,1:T(8,128)(2,1)}, u32[]{:S(2)}) copy-start(bf16[2048,2,128]{2,0,1:T(8,128)(2,1)} %get-tuple-element.205) | copy-start | bytes 3145732 | tf_op jit(solution)/shard_map/while
  277.2 3.4 copy-start.9
  280.6 5.5 %copy-start.4 = (bf16[2048,2,128]{2,0,1:T(8,128)(2,1)S(1)}, bf16[2048,2,128]{2,0,1:T(8,128)(2,1)}, u32[]{:S(2)}) copy-start(bf16[2048,2,128]{2,0,1:T(8,128)(2,1)} %get-tuple-element.202) | copy-start | bytes 3145732 | tf_op jit(solution)/shard_map/while
  286.1 4.5 %copy-start.5 = (bf16[2048,2,128]{2,0,1:T(8,128)(2,1)S(1)}, bf16[2048,2,128]{2,0,1:T(8,128)(2,1)}, u32[]{:S(2)}) copy-start(bf16[2048,2,128]{2,0,1:T(8,128)(2,1)} %get-tuple-element.205) | copy-start | bytes 3145732 | tf_op jit(solution)/shard_map/while
  294.8 7.6 %copy-start.6 = (bf16[4,512,2,128]{3,1,0,2:T(8,128)(2,1)S(1)}, bf16[4,512,2,128]{3,1,0,2:T(8,128)(2,1)}, u32[]{:S(2)}) copy-start(bf16[4,512,2,128]{3,1,0,2:T(8,128)(2,1)} %get-tuple-element.56) | copy-start | bytes 3145732
  298.5 20.1 %all-to-all-start.6 = ((bf16[2048,1,2,128]{3,2,1,0:T(2,128)(2,1)}), bf16[2048,1,2,128]{3,2,1,0:T(2,128)(2,1)S(1)}, u32[]{:S(2)}, u32[]{:S(2)}) async-start(bf16[2048,1,2,128]{3,2,1,0:T(2,128)(2,1)} %copy.65), calls=%async_computation.6 | async-start | bytes 2097152 | tf_op jit(solution)/shard_map/all_to_all | solution.py:97
  318.6 20.1 %all-to-all-start.7 = ((bf16[2048,1,2,128]{3,2,1,0:T(2,128)(2,1)}), bf16[2048,1,2,128]{3,2,1,0:T(2,128)(2,1)S(1)}, u32[]{:S(2)}, u32[]{:S(2)}) async-start(bf16[2048,1,2,128]{3,2,1,0:T(2,128)(2,1)} %copy.69), calls=%async_computation.7 | async-start | bytes 2097152 | tf_op jit(solution)/shard_map/all_to_all | solution.py:98
where the time goes:
time: 343 us; the launch traced here: 341 us
  matrix products  89 us (26%)
  waiting for transfers between devices  84.2 us (25%)
  blocking collectives  61.8 us (18%)
  local copies, waits for them, and re-layouts  56.9 us (17%)
  starting transfers between devices  35.3 us (10%)
  loops' own time  7.68 us (2%)
  other arithmetic  5.06 us (1%)
    all_gather x1, blocking collectives, on_device(): lax.all_gather(key_gain, 'clip', axis=0, tiled=True)  31.2 us
    all_gather x1, blocking collectives, on_device(): lax.all_gather(query_gain, 'clip', axis=0, tiled=True)  30.6 us
    sub x4, matrix products, one_block(): weights = jnp.exp(scores - top)  27.3 us
    dot_general x4, matrix products, one_block(): jnp.einsum('qhd,khd->hqk', query_blk, keys_d, preferred_element_type=jnp....  22.1 us
    dot_general x4, matrix products, one_block(): jnp.einsum('hqk,khd->qhd', weights_tan_low, vals, preferred_element_type=...  18.2 us
    all_to_all x1, waiting for transfers between devices, on_device(): lax.all_to_all(split_heads(query_norm), 'seq', split_axis=1, concat_axis=...  15.1 us
    all_to_all x1, waiting for transfers between devices, on_device(): lax.all_to_all(outs_tan, 'seq', split_axis=0, concat_axis=1, tiled=True)  14.3 us
    all_to_all x1, waiting for transfers between devices, on_device(): lax.all_to_all(split_heads(query_norm_tan), 'seq', split_axis=1, concat_a...  13.5 us
  transfers between devices with their start and end apart: 8, of which 7 were waited for; matrix products, arithmetic and copies ran while one was open for 10% of the time, Pallas kernels for 0%

commit v1 on v0

v1 whole, which is shorter than its diff:
```python
import functools

import jax
import jax.numpy as jnp
from jax import lax
from jax.experimental import pallas as pl
from jax.experimental.pallas import tpu as pltpu
from jax.sharding import PartitionSpec as P

HEADS = 32
HD = 128
EPS = 1e-06
LOG2E = 1.4426950408889634
MESH = pl.DeviceIdType.MESH
F32 = jnp.float32
BF16 = jnp.bfloat16

CHIPS = ((1, 0), (3, 0), (0, 1), (2, 0), (1, 1), (3, 1), (2, 1))
PEERS = tuple((x, y, 0) for x, y in CHIPS) + tuple((x, y, 1) for x, y in CHIPS) + ((0, 0, 1),)


def digit(table, index):
    code = sum(v * 4**i for i, v in enumerate(table))
    return (code // 4**index) % 4 if isinstance(index, int) else lax.rem(lax.shift_right_logical(jnp.int32(code), 2 * index), 4)


def kernel(clips, q_hbm, k_hbm, v_hbm, qt_hbm, kt_hbm, vt_hbm, gq_hbm, gk_hbm, o_hbm, ot_hbm,
           raw, normed, gains, vbuf, vcat, kbuf, qbuf, obuf,
           load_sem, gain_send, gain_recv, v_send, v_recv, k_send, k_recv, q_send, q_recv, o_send, o_recv):
    clip = lax.axis_index("clip")
    me = lax.axis_index("seq")
    x, y, core = me // 4, (me // 2) % 2, me % 2
    tok, width = q_hbm.shape
    groups = HEADS // 2
    length = groups * tok
    pair = 2 * HD

    def at(offset):
        return ((x + offset[0]) % 4) * 4 + ((y + offset[1]) % 2) * 2 + (core + offset[2]) % 2

    def columns(index, size):
        return pl.ds(pl.multiple_of(index * size, size), size)

    loads = [pltpu.make_async_copy(src, raw.at[i], load_sem.at[i]) for i, src in enumerate((k_hbm, kt_hbm, q_hbm, qt_hbm))]
    for copy in loads:
        copy.start()

    barrier = pltpu.get_barrier_semaphore()
    for offset in PEERS:
        pl.semaphore_signal(barrier, inc=1, device_id=(clip, at(offset)), device_id_type=MESH)
    for step in range(1, clips):
        pl.semaphore_signal(barrier, inc=1, device_id=((clip + step) % clips, me), device_id_type=MESH)
    pl.semaphore_wait(barrier, len(PEERS) + clips - 1)

    mine = columns(me, tok)
    for step in range(1, clips):
        for i, src in enumerate((gk_hbm, gq_hbm)):
            pltpu.make_async_remote_copy(
                src_ref=src, dst_ref=gains.at[i, clip], send_sem=gain_send.at[i], recv_sem=gain_recv,
                device_id=((clip + step) % clips, me), device_id_type=MESH).start()
    for offset in PEERS:
        to = at(offset)
        for i, src in enumerate((v_hbm, vt_hbm)):
            pltpu.make_async_remote_copy(
                src_ref=src.at[:, columns(to, pair)], dst_ref=vbuf.at[i, mine, :], send_sem=v_send.at[i], recv_sem=v_recv,
                device_id=(clip, to), device_id_type=MESH).start()
    for i, src in enumerate((gk_hbm, gq_hbm)):
        pltpu.make_async_copy(src, gains.at[i, clip], gain_recv).start()
    for i, src in enumerate((v_hbm, vt_hbm)):
        pltpu.make_async_copy(src.at[:, columns(me, pair)], vbuf.at[i, mine, :], v_recv).start()
    pltpu.make_async_copy(gains, gains, gain_recv).wait()

    def norm(i, tangent_first):
        first, second = (1, 0) if tangent_first else (0, 1)

        def rows(n, _):
            r = pl.ds(pl.multiple_of(n * 16, 16), 16)
            square, cross = jnp.zeros((16, HD), F32), jnp.zeros((16, HD), F32)
            for h in range(HEADS):
                a = raw[2 * i, r, h * HD:(h + 1) * HD].astype(F32)
                b = raw[2 * i + 1, r, h * HD:(h + 1) * HD].astype(F32)
                square += a * a
                cross += a * b
            inverse = 1.0 / jnp.sqrt(jnp.sum(square, axis=1, keepdims=True) / width + EPS)
            mixed = jnp.sum(cross, axis=1, keepdims=True) / width * (inverse * inverse * inverse)
            per = gains.shape[-1] // HD
            for h in range(HEADS):
                a = raw[2 * i, r, h * HD:(h + 1) * HD].astype(F32)
                b = raw[2 * i + 1, r, h * HD:(h + 1) * HD].astype(F32)
                g = gains[i, h // per, :, (h % per) * HD:(h % per + 1) * HD]
                normed[i, r, (2 * h + first) * HD:(2 * h + first + 1) * HD] = (g * a * inverse).astype(BF16)
                normed[i, r, (2 * h + second) * HD:(2 * h + second + 1) * HD] = (g * (b * inverse - a * mixed)).astype(BF16)
            return 0

        lax.fori_loop(0, tok // 16, rows, 0)

    loads[0].wait()
    loads[1].wait()
    norm(0, False)
    for offset in PEERS:
        to = at(offset)
        pltpu.make_async_remote_copy(
            src_ref=normed.at[0, :, columns(to, 2 * pair)], dst_ref=kbuf.at[mine, :], send_sem=k_send, recv_sem=k_recv,
            device_id=(clip, to), device_id_type=MESH).start()
    pltpu.make_async_copy(normed.at[0, :, columns(me, 2 * pair)], kbuf.at[mine, :], k_recv).start()
    loads[2].wait()
    loads[3].wait()
    norm(1, True)
    for offset in PEERS:
        to = at(offset)
        pltpu.make_async_remote_copy(
            src_ref=normed.at[1, :, columns(to, 2 * pair)], dst_ref=qbuf.at[mine, :], send_sem=q_send, recv_sem=q_recv.at[me],
            device_id=(clip, to), device_id_type=MESH).start()
    pltpu.make_async_copy(normed.at[1, :, columns(me, 2 * pair)], qbuf.at[mine, :], q_recv.at[me]).start()

    pltpu.make_async_copy(vbuf, vbuf, v_recv).wait()

    def interleave(n, _):
        r = pl.ds(pl.multiple_of(n * 128, 128), 128)
        for h in range(2):
            for i in range(2):
                vcat[r, (2 * h + i) * HD:(2 * h + i + 1) * HD] = vbuf[i, r, h * HD:(h + 1) * HD]
        return 0

    lax.fori_loop(0, length // 128, interleave, 0)
    pltpu.make_async_copy(kbuf, kbuf, k_recv).wait()

    scale = HD ** (-0.5)
    order = tuple(((4 - dx) % 4, dy) for dx, dy in CHIPS) + ((0, 0),)

    def attend(t, _):
        chip = ((x + digit([o[0] for o in order], t)) % 4) * 2 + (y + digit([o[1] for o in order], t)) % 2
        r = pl.ds(pl.multiple_of(chip * 2 * tok, 2 * tok), 2 * tok)
        for c in range(2):
            owner = chip * 2 + c
            block = qbuf.at[columns(owner, tok), :]
            pltpu.make_async_copy(block, block, q_recv.at[owner]).wait()
        for h in range(2):
            cols = slice(h * pair, (h + 1) * pair)
            queries = qbuf[r, cols]
            keys = kbuf[:, cols]
            dims = (((1,), (1,)), ((), ()))
            scores = lax.dot_general(queries[:, HD:], keys[:, :HD], dims, preferred_element_type=F32)
            scores_tan = lax.dot_general(queries, keys, dims, preferred_element_type=F32)
            top = jnp.max(scores, axis=1, keepdims=True)
            weights = jnp.exp2((scores - top) * (scale * LOG2E))
            inverse = 1.0 / jnp.sum(weights, axis=1, keepdims=True)
            mean = jnp.sum(weights * scores_tan, axis=1, keepdims=True) * inverse
            low = (weights * inverse).astype(BF16)
            low_tan = (weights * (scores_tan - mean) * (inverse * scale)).astype(BF16)
            both = jnp.dot(low, vcat[:, cols], preferred_element_type=F32)
            rest = jnp.dot(low_tan, vcat[:, h * pair:h * pair + HD], preferred_element_type=F32)
            obuf[0, r, h * HD:(h + 1) * HD] = both[:, :HD].astype(BF16)
            obuf[1, r, h * HD:(h + 1) * HD] = (both[:, HD:] + rest).astype(BF16)
        for c in range(2):
            owner = chip * 2 + c
            for i, out in enumerate((o_hbm, ot_hbm)):
                block = obuf.at[i, columns(owner, tok), :]
                place = out.at[:, columns(me, pair)]

                @pl.when(owner != me)
                def _():
                    pltpu.make_async_remote_copy(
                        src_ref=block, dst_ref=place, send_sem=o_send.at[i], recv_sem=o_recv.at[i],
                        device_id=(clip, owner), device_id_type=MESH).start()

                @pl.when(owner == me)
                def _():
                    pltpu.make_async_copy(block, place, o_recv.at[i]).start()
        return 0

    lax.fori_loop(0, groups // 2, attend, 0)

    for i, out in enumerate((o_hbm, ot_hbm)):
        pltpu.make_async_copy(out, out, o_recv.at[i]).wait()
    others = pl.ds(0, length - tok)
    for i in range(2):
        pltpu.make_async_copy(vbuf.at[i, others, :], vbuf.at[i, others, :], v_send.at[i]).wait()
        pltpu.make_async_copy(obuf.at[i, others, :], obuf.at[i, others, :], o_send.at[i]).wait()
        pltpu.make_async_copy(gains.at[i, pl.ds(0, clips - 1)], gains.at[i, pl.ds(0, clips - 1)], gain_send.at[i]).wait()
    pltpu.make_async_copy(kbuf.at[others, :], kbuf.at[others, :], k_send).wait()
    pltpu.make_async_copy(qbuf.at[others, :], qbuf.at[others, :], q_send).wait()


def on_device(query_raw, key_raw, values, query_tan, key_tan, values_tan, query_gain, key_gain):
    tok, width = query_raw.shape
    groups = lax.axis_size("seq")
    clips = lax.axis_size("clip")
    length = tok * groups
    share = query_gain.shape[0]
    dma = pltpu.SemaphoreType.DMA
    anywhere = pl.BlockSpec(memory_space=pl.ANY)
    return pl.pallas_call(
        functools.partial(kernel, clips),
        out_shape=(jax.ShapeDtypeStruct((tok, width), BF16),) * 2,
        in_specs=[anywhere] * 8,
        out_specs=(anywhere,) * 2,
        scratch_shapes=[
            pltpu.VMEM((4, tok, width), BF16),
            pltpu.VMEM((2, tok, 2 * width), BF16),
            pltpu.VMEM((2, clips, 1, share), F32),
            pltpu.VMEM((2, length, 2 * HD), BF16),
            pltpu.VMEM((length, 4 * HD), BF16),
            pltpu.VMEM((length, 4 * HD), BF16),
            pltpu.VMEM((length, 4 * HD), BF16),
            pltpu.VMEM((2, length, 2 * HD), BF16),
            dma((4,)), dma((2,)), dma, dma((2,)), dma, dma, dma, dma, dma((groups,)), dma((2,)), dma((2,)),
        ],
        compiler_params=pltpu.CompilerParams(
            collective_id=0, has_side_effects=True, vmem_limit_bytes=56 * 2**20
        ),
        cost_estimate=pl.CostEstimate(flops=13_000_000_000, bytes_accessed=8 * 2**20, transcendentals=8_400_000),
    )(query_raw, key_raw, values, query_tan, key_tan, values_tan,
      query_gain.reshape(1, share), key_gain.reshape(1, share))


def solution(mesh):
    tokens = P(("clip", "seq"), None)
    return jax.shard_map(
        on_device, mesh=mesh, in_specs=(tokens,) * 6 + (P("clip"),) * 2, out_specs=(tokens,) * 2, check_vma=False
    )
```

time: 343 us -> 114 us (0.33)
  the two profiles are of different devices: /device:TPU:0 before, /device:TPU:103 now
where the time goes in v1:
time: 114 us
  Pallas kernels  110 us (96%)
  local copies, waits for them, and re-layouts  3.35 us (3%)
    pallas_call x1, Pallas kernels, on_device(): pl.pallas_call(functools.partial(kernel, clips), out_shape=(jax.ShapeDtyp...  110 us
    unnamed x4, local copies, waits for them, and re-layouts  3.35 us

profile of v1, /device:TPU:103, one launch (start us, length us, event | category | flops | bytes accessed | tf_op | source)
XLA Modules:
  0.0 114.0 jit_solution(13954445720806607790)
XLA Ops:
  0.6 110.0 %shard_map.95 = (bf16[128,4096]{1,0:T(8,128)(2,1)}, bf16[128,4096]{1,0:T(8,128)(2,1)}) custom-call(bf16[128,4096]{1,0:T(8,128)(2,1)} %q_hbm.1, bf16[128,4096]{1,0:T(8,128)(2,1)} %k_hbm.1, bf16[128,4096]{1,0:T(8,128)(2,1)} %v_hbm.1, bf16[128,4096]{1,0:T(8,128)(2,1)} %qt_hbm.1, bf16[128,4096]{1,0:T(8,128)(2,1)} %kt_hbm.1, bf16[128,4096]{1,0:T(8,128)(2,1)} %vt_hbm.1, ...), custom_call_target="tpu_custom_call" | custom-call | flops 12999999488 | bytes 8388608 | tf_op jit(solution)/shard_map/pallas_call | solution.py:193
  110.6 0.0 copy-start
  110.6 2.4 %copy.12 = bf16[128,4096]{1,0:T(8,128)(2,1)} copy(bf16[128,4096]{1,0:T(8,128)(2,1)} %get-tuple-element.4) | data formatting | bytes 2097152
  113.0 0.0 copy-done
  113.0 1.0 copy.13
Async XLA Ops:
  110.6 2.4 %copy-start = (bf16[128,4096]{1,0:T(8,128)(2,1)S(1)}, bf16[128,4096]{1,0:T(8,128)(2,1)}, u32[]{:S(2)}) copy-start(bf16[128,4096]{1,0:T(8,128)(2,1)} %get-tuple-element.5) | copy-start | bytes 3145732

commit v2 on v1

v2 whole, which is shorter than its diff:
```python
import functools

import jax
import jax.numpy as jnp
from jax import lax
from jax.experimental import pallas as pl
from jax.experimental.pallas import tpu as pltpu
from jax.sharding import PartitionSpec as P

HEADS = 32
HD = 128
EPS = 1e-06
LOG2E = 1.4426950408889634
MESH = pl.DeviceIdType.MESH
F32 = jnp.float32
BF16 = jnp.bfloat16

NEAR = ((1, 0), (3, 0), (0, 1), (2, 0))
FAR = ((1, 1), (3, 1), (2, 1), (0, 0))
PLACES = tuple((dx, dy, core) for chips in (NEAR, FAR) for core in range(2) for dx, dy in chips)
OWN = PLACES.index((0, 0, 0))
OTHERS = tuple(p for p in range(16) if p != OWN)
PARTS = 2
CHUNKS = 4


def kernel(clips, q_hbm, k_hbm, v_hbm, qt_hbm, kt_hbm, vt_hbm, gq_hbm, gk_hbm, out_hbm,
           raw, normed, gains, vbuf, vcat, kbuf, qbuf, obuf,
           load_sem, gain_send, gain_recv, v_send, v_recv, k_send, k_recv, q_send, q_recv, o_send, o_recv):
    clip = lax.axis_index("clip")
    me = lax.axis_index("seq")
    x, y, core = me // 4, (me // 2) % 2, me % 2
    way = 1 - 2 * (x % 2)
    tok, width = q_hbm.shape
    groups = HEADS // 2
    length = groups * tok
    pair = 2 * HD
    piece = tok // PARTS

    def at(place):
        dx, dy, other = PLACES[place]
        return ((x + way * dx + 4) % 4) * 4 + ((y + dy) % 2) * 2 + (core + other) % 2

    def columns(index, size):
        return pl.ds(pl.multiple_of(index * size, size), size)

    loads = [pltpu.make_async_copy(src, raw.at[i], load_sem.at[i]) for i, src in enumerate((k_hbm, kt_hbm, q_hbm, qt_hbm))]
    for copy in loads:
        copy.start()

    barrier = pltpu.get_barrier_semaphore()
    for place in OTHERS:
        pl.semaphore_signal(barrier, inc=1, device_id=(clip, at(place)), device_id_type=MESH)
    for step in range(1, clips):
        pl.semaphore_signal(barrier, inc=1, device_id=((clip + step) % clips, me), device_id_type=MESH)
    pl.semaphore_wait(barrier, len(OTHERS) + clips - 1)

    for step in range(1, clips):
        for i, src in enumerate((gk_hbm, gq_hbm)):
            pltpu.make_async_remote_copy(
                src_ref=src, dst_ref=gains.at[i, clip], send_sem=gain_send.at[i], recv_sem=gain_recv,
                device_id=((clip + step) % clips, me), device_id_type=MESH).start()
    for i, src in enumerate((v_hbm, vt_hbm)):
        for place in OTHERS:
            to = at(place)
            pltpu.make_async_remote_copy(
                src_ref=src.at[:, columns(to, pair)], dst_ref=vbuf.at[i, pl.ds(place * tok, tok), :], send_sem=v_send.at[i], recv_sem=v_recv,
                device_id=(clip, to), device_id_type=MESH).start()
    for i, src in enumerate((gk_hbm, gq_hbm)):
        pltpu.make_async_copy(src, gains.at[i, clip], gain_recv).start()
    for i, src in enumerate((v_hbm, vt_hbm)):
        pltpu.make_async_copy(src.at[:, columns(me, pair)], vbuf.at[i, pl.ds(OWN * tok, tok), :], v_recv).start()
    pltpu.make_async_copy(gains, gains, gain_recv).wait()

    def norm(i, tangent_first):
        first, second = (1, 0) if tangent_first else (0, 1)

        def rows(n, _):
            r = pl.ds(pl.multiple_of(n * 16, 16), 16)
            square, cross = jnp.zeros((16, HD), F32), jnp.zeros((16, HD), F32)
            for h in range(HEADS):
                a = raw[2 * i, r, h * HD:(h + 1) * HD].astype(F32)
                b = raw[2 * i + 1, r, h * HD:(h + 1) * HD].astype(F32)
                square += a * a
                cross += a * b
            inverse = 1.0 / jnp.sqrt(jnp.sum(square, axis=1, keepdims=True) / width + EPS)
            mixed = jnp.sum(cross, axis=1, keepdims=True) / width * (inverse * inverse * inverse)
            per = gains.shape[-1] // HD
            for h in range(HEADS):
                a = raw[2 * i, r, h * HD:(h + 1) * HD].astype(F32)
                b = raw[2 * i + 1, r, h * HD:(h + 1) * HD].astype(F32)
                g = gains[i, h // per, :, (h % per) * HD:(h % per + 1) * HD]
                normed[i, r, (2 * h + first) * HD:(2 * h + first + 1) * HD] = (g * a * inverse).astype(BF16)
                normed[i, r, (2 * h + second) * HD:(2 * h + second + 1) * HD] = (g * (b * inverse - a * mixed)).astype(BF16)
            return 0

        lax.fori_loop(0, tok // 16, rows, 0)

    loads[0].wait()
    loads[1].wait()
    norm(0, False)
    for head in range(2):
        for place in OTHERS:
            to = at(place)
            pltpu.make_async_remote_copy(
                src_ref=normed.at[0, :, columns(2 * to + head, pair)], dst_ref=kbuf.at[head, pl.ds(place * tok, tok), :],
                send_sem=k_send, recv_sem=k_recv, device_id=(clip, to), device_id_type=MESH).start()
    for head in range(2):
        pltpu.make_async_copy(
            normed.at[0, :, columns(2 * me + head, pair)], kbuf.at[head, pl.ds(OWN * tok, tok), :], k_recv).start()
    loads[2].wait()
    loads[3].wait()
    norm(1, True)
    for part in range(PARTS):
        rows = pl.ds(part * piece, piece)
        for place in range(16):
            to = at(place)
            block = normed.at[1, rows, columns(to, 2 * pair)]
            there = qbuf.at[part, place // 4, pl.ds(place % 4 * piece, piece), :]
            if place == OWN:
                pltpu.make_async_copy(block, there, q_recv.at[part, place]).start()
            else:
                pltpu.make_async_remote_copy(
                    src_ref=block, dst_ref=there, send_sem=q_send, recv_sem=q_recv.at[part, place],
                    device_id=(clip, to), device_id_type=MESH).start()

    pltpu.make_async_copy(vbuf, vbuf, v_recv).wait()

    def interleave(n, _):
        r = pl.ds(pl.multiple_of(n * 128, 128), 128)
        for h in range(2):
            for i in range(2):
                vcat[r, (2 * h + i) * HD:(2 * h + i + 1) * HD] = vbuf[i, r, h * HD:(h + 1) * HD]
        return 0

    lax.fori_loop(0, length // 128, interleave, 0)
    pltpu.make_async_copy(kbuf, kbuf, k_recv).wait()

    scale = HD ** (-0.5)
    def attend(step, _):
        part, group = step // 4, step % 4
        for n in range(4):
            block = qbuf.at[part, group, pl.ds(n * piece, piece), :]
            pltpu.make_async_copy(block, block, q_recv.at[part, group * 4 + n]).wait()
        for h in range(2):
            queries = qbuf[part, group, :, h * pair:(h + 1) * pair]
            keys = kbuf[h]
            dims = (((1,), (1,)), ((), ()))
            scores = lax.dot_general(queries[:, HD:], keys[:, :HD], dims, preferred_element_type=F32)
            scores_tan = lax.dot_general(queries, keys, dims, preferred_element_type=F32)
            top = jnp.max(scores, axis=1, keepdims=True)
            weights = jnp.exp2((scores - top) * (scale * LOG2E))
            inverse = 1.0 / jnp.sum(weights, axis=1, keepdims=True)
            mean = jnp.sum(weights * scores_tan, axis=1, keepdims=True) * inverse
            low = (weights * inverse).astype(BF16)
            low_tan = (weights * (scores_tan - mean) * (inverse * scale)).astype(BF16)
            both = jnp.dot(low, vcat[:, h * pair:(h + 1) * pair], preferred_element_type=F32)
            rest = jnp.dot(low_tan, vcat[:, h * pair:h * pair + HD], preferred_element_type=F32)
            obuf[step, 0, :, h * HD:(h + 1) * HD] = both[:, :HD].astype(BF16)
            obuf[step, 1, :, h * HD:(h + 1) * HD] = (both[:, HD:] + rest).astype(BF16)
        far, other = group // 2, group % 2
        rows = pl.ds(pl.multiple_of(part * piece, piece), piece)
        for n in range(4):
            dx = NEAR[n][0] + far * (FAR[n][0] - NEAR[n][0])
            dy = NEAR[n][1] + far * (FAR[n][1] - NEAR[n][1])
            owner = ((x + way * dx + 4) % 4) * 4 + ((y + dy) % 2) * 2 + (core + other) % 2
            block = obuf.at[step, :, pl.ds(n * piece, piece), :]
            there = out_hbm.at[:, rows, columns(me, pair)]

            def send(block=block, there=there, owner=owner):
                pltpu.make_async_remote_copy(
                    src_ref=block, dst_ref=there, send_sem=o_send, recv_sem=o_recv,
                    device_id=(clip, owner), device_id_type=MESH).start()

            if n == OWN % 4:
                pl.when(group != OWN // 4)(send)

                @pl.when(group == OWN // 4)
                def _():
                    pltpu.make_async_copy(block, there, o_recv).start()
            else:
                send()
        return 0

    lax.fori_loop(0, PARTS * 4, attend, 0)

    pltpu.make_async_copy(out_hbm, out_hbm, o_recv).wait()
    others = pl.ds(0, length - tok)
    for i in range(2):
        pltpu.make_async_copy(vbuf.at[i, others, :], vbuf.at[i, others, :], v_send.at[i]).wait()
        pltpu.make_async_copy(gains.at[i, pl.ds(0, clips - 1)], gains.at[i, pl.ds(0, clips - 1)], gain_send.at[i]).wait()
    pltpu.make_async_copy(kbuf.at[:, others, :], kbuf.at[:, others, :], k_send).wait()
    most = pl.ds(0, 4 * piece - piece // 4)
    pltpu.make_async_copy(qbuf.at[:, :, most, :], qbuf.at[:, :, most, :], q_send).wait()
    pltpu.make_async_copy(obuf.at[:, :, most, :], obuf.at[:, :, most, :], o_send).wait()


def hand_out(both, first, second, buf, in_sems, out_sems):
    pieces, rows = buf.shape[0] // 2, buf.shape[1]
    copies = []
    for n in range(pieces):
        for i, out in enumerate((first, second)):
            k, r = 2 * n + i, pl.ds(n * rows, rows)
            copies.append((pltpu.make_async_copy(both.at[i, r, :], buf.at[k], in_sems.at[k]),
                           pltpu.make_async_copy(buf.at[k], out.at[r, :], out_sems.at[k])))
    for fetch, _ in copies:
        fetch.start()
    for fetch, store in copies:
        fetch.wait()
        store.start()
    for _, store in copies:
        store.wait()


def on_device(query_raw, key_raw, values, query_tan, key_tan, values_tan, query_gain, key_gain):
    tok, width = query_raw.shape
    groups = lax.axis_size("seq")
    clips = lax.axis_size("clip")
    length = tok * groups
    share = query_gain.shape[0]
    dma = pltpu.SemaphoreType.DMA
    anywhere = pl.BlockSpec(memory_space=pl.ANY)
    both = pl.pallas_call(
        functools.partial(kernel, clips),
        out_shape=jax.ShapeDtypeStruct((2, tok, width), BF16),
        in_specs=[anywhere] * 8,
        out_specs=anywhere,
        scratch_shapes=[
            pltpu.VMEM((4, tok, width), BF16),
            pltpu.VMEM((2, tok, 2 * width), BF16),
            pltpu.VMEM((2, clips, 1, share), F32),
            pltpu.VMEM((2, length, 2 * HD), BF16),
            pltpu.VMEM((length, 4 * HD), BF16),
            pltpu.VMEM((2, length, 2 * HD), BF16),
            pltpu.VMEM((PARTS, 4, length // PARTS // 4, 4 * HD), BF16),
            pltpu.VMEM((PARTS * 4, 2, length // PARTS // 4, 2 * HD), BF16),
            dma((4,)), dma((2,)), dma, dma((2,)), dma, dma, dma, dma, dma((PARTS, groups)), dma, dma,
        ],
        compiler_params=pltpu.CompilerParams(
            collective_id=0, has_side_effects=True, vmem_limit_bytes=56 * 2**20
        ),
        cost_estimate=pl.CostEstimate(flops=13_000_000_000, bytes_accessed=8 * 2**20, transcendentals=8_400_000),
    )(query_raw, key_raw, values, query_tan, key_tan, values_tan,
      query_gain.reshape(1, share), key_gain.reshape(1, share))
    return pl.pallas_call(
        hand_out,
        out_shape=(jax.ShapeDtypeStruct((tok, width), BF16),) * 2,
        in_specs=[anywhere],
        out_specs=(anywhere,) * 2,
        scratch_shapes=[pltpu.VMEM((2 * CHUNKS, tok // CHUNKS, width), BF16), dma((2 * CHUNKS,)), dma((2 * CHUNKS,))],
    )(both)


def solution(mesh):
    tokens = P(("clip", "seq"), None)
    return jax.shard_map(
        on_device, mesh=mesh, in_specs=(tokens,) * 6 + (P("clip"),) * 2, out_specs=(tokens,) * 2, check_vma=False
    )
```

time: 114 us -> 107 us (0.939)
  the two profiles are of different devices: /device:TPU:103 before, /device:TPU:0 now
where the time goes in v2:
time: 107 us; the launch traced here: 105 us
  Pallas kernels  104 us (97%)
    pallas_call x1, Pallas kernels, on_device(): pl.pallas_call(functools.partial(kernel, clips), out_shape=jax.ShapeDtype...  102 us
    pallas_call x1, Pallas kernels, on_device(): pl.pallas_call(hand_out, out_shape=(jax.ShapeDtypeStruct((tok, width), BF...  2.4 us

profile of v2, /device:TPU:0, one launch (start us, length us, event | category | flops | bytes accessed | tf_op | source)
XLA Modules:
  0.0 105.0 jit_solution(2537390259617933978)
XLA Ops:
  0.6 102.0 %shard_map.95.both = bf16[2,128,4096]{2,1,0:T(8,128)(2,1)} custom-call(bf16[128,4096]{1,0:T(8,128)(2,1)} %q_hbm.1, bf16[128,4096]{1,0:T(8,128)(2,1)} %k_hbm.1, bf16[128,4096]{1,0:T(8,128)(2,1)} %v_hbm.1, bf16[128,4096]{1,0:T(8,128)(2,1)} %qt_hbm.1, bf16[128,4096]{1,0:T(8,128)(2,1)} %kt_hbm.1, bf16[128,4096]{1,0:T(8,128)(2,1)} %vt_hbm.1, f32[1,512]{1,0:T(1,128)} %bitcast.2, ...), custom_call_target="tpu_custom_call" | custom-call | flops 12999999488 | bytes 8388608 | tf_op jit(solution)/shard_map/pallas_call | solution.py:223
  102.6 2.4 %shard_map.96 = (bf16[128,4096]{1,0:T(8,128)(2,1)}, bf16[128,4096]{1,0:T(8,128)(2,1)}) custom-call(bf16[2,128,4096]{2,1,0:T(8,128)(2,1)} %shard_map.95.both), custom_call_target="tpu_custom_call" | custom-call | tf_op jit(solution)/shard_map/pallas_call | solution.py:245

commit v3 on v2

v3 whole, which is shorter than its diff:
```python
import functools

import jax
import jax.numpy as jnp
from jax import lax
from jax.experimental import pallas as pl
from jax.experimental.pallas import tpu as pltpu
from jax.sharding import PartitionSpec as P

HEADS = 32
HD = 128
EPS = 1e-06
LOG2E = 1.4426950408889634
MESH = pl.DeviceIdType.MESH
F32 = jnp.float32
BF16 = jnp.bfloat16

FAR = ((2, 1), (3, 1), (1, 1), (0, 0))
NEAR = ((0, 1), (2, 0), (3, 0), (1, 0))
PLACES = tuple((dx, dy, core) for core in range(2) for chips in (FAR, NEAR) for dx, dy in chips)
OWN = PLACES.index((0, 0, 0))
OTHERS = tuple(p for p in range(16) if p != OWN)
PARTS = 2
RELAY = 0


def kernel(clips, q_hbm, k_hbm, v_hbm, qt_hbm, kt_hbm, vt_hbm, gq_hbm, gk_hbm, out_hbm,
           queries, keys, figures, figure_mine, figure_all, figure_of, gains, gain,
           vbuf, vcat, kraw, kbuf, qbuf, obuf,
           load_k, load_q, gain_send, gain_recv, hand_send, hand_recv, figure_send, figure_recv,
           v_send, v_recv, k_send, k_recv, q_send, q_recv, o_send, o_recv):
    clip = lax.axis_index("clip")
    me = lax.axis_index("seq")
    x, y, core = me // 4, (me // 2) % 2, me % 2
    way = 1 - 2 * (x % 2)
    tok, width = q_hbm.shape
    groups = HEADS // 2
    length = groups * tok
    pair = 2 * HD
    piece = tok // PARTS
    share = gains.shape[-1]

    def at(place):
        dx, dy, other = PLACES[place]
        return ((x + way * dx + 4) % 4) * 4 + ((y + dy) % 2) * 2 + (core + other) % 2

    def columns(index, size):
        return pl.ds(pl.multiple_of(index * size, size), size)

    def send(src, dst, send_sem, recv_sem, to):
        pltpu.make_async_remote_copy(
            src_ref=src, dst_ref=dst, send_sem=send_sem, recv_sem=recv_sem, device_id=(clip, to), device_id_type=MESH).start()

    for i, src in enumerate((k_hbm, kt_hbm)):
        pltpu.make_async_copy(src, keys.at[i], load_k).start()
    for n in range(groups):
        for i, src in enumerate((qt_hbm, q_hbm)):
            pltpu.make_async_copy(
                src.at[:, n * pair:(n + 1) * pair], queries.at[:, (2 * n + i) * pair:(2 * n + i + 1) * pair], load_q).start()

    barrier = pltpu.get_barrier_semaphore()
    for place in OTHERS:
        pl.semaphore_signal(barrier, inc=1, device_id=(clip, at(place)), device_id_type=MESH)

    @pl.when(me == RELAY)
    def _():
        for step in range(1, clips):
            pl.semaphore_signal(barrier, inc=1, device_id=((clip + step) % clips, me), device_id_type=MESH)

    @pl.when(me != RELAY)
    def _():
        pl.semaphore_wait(barrier, len(OTHERS))

    @pl.when(me == RELAY)
    def _():
        pl.semaphore_wait(barrier, len(OTHERS) + clips - 1)
        for i, src in enumerate((gk_hbm, gq_hbm)):
            for step in range(1, clips):
                pltpu.make_async_remote_copy(
                    src_ref=src, dst_ref=gains.at[i, clip], send_sem=gain_send.at[i], recv_sem=gain_recv,
                    device_id=((clip + step) % clips, me), device_id_type=MESH).start()
            pltpu.make_async_copy(src, gains.at[i, clip], gain_recv).start()

    for i, src in enumerate((v_hbm, vt_hbm)):
        for place in OTHERS:
            to = at(place)
            send(src.at[:, columns(to, pair)], vbuf.at[i, pl.ds(place * tok, tok), :], v_send.at[i], v_recv, to)
        pltpu.make_async_copy(src.at[:, columns(me, pair)], vbuf.at[i, pl.ds(OWN * tok, tok), :], v_recv).start()

    pltpu.make_async_copy(keys, keys, load_k).wait()
    pltpu.make_async_copy(queries, queries, load_q).wait()

    def token_figures(n, _):
        r = pl.ds(pl.multiple_of(n * 16, 16), 16)

        def pair_of(primal, tangent):
            square, cross = jnp.zeros((16, HD), F32), jnp.zeros((16, HD), F32)
            for h in range(HEADS):
                a, b = primal(h).astype(F32), tangent(h).astype(F32)
                square += a * a
                cross += a * b
            inverse = 1.0 / jnp.sqrt(jnp.sum(square, axis=1, keepdims=True) / width + EPS)
            return inverse, jnp.sum(cross, axis=1, keepdims=True) / width * (inverse * inverse * inverse)

        def query_part(i):
            def part(h):
                start = (2 * (h // 2) + i) * pair + h % 2 * HD
                return queries[r, start:start + HD]
            return part

        found = pair_of(query_part(1), query_part(0)) + pair_of(
            lambda h: keys[0, r, h * HD:(h + 1) * HD], lambda h: keys[1, r, h * HD:(h + 1) * HD])
        lane = lax.broadcasted_iota(jnp.int32, (16, HD), 1)
        row = jnp.zeros((16, HD), F32)
        for i, value in enumerate(found):
            row = jnp.where(lane == i, value, row)
        figures[r, :] = row
        return 0

    lax.fori_loop(0, tok // 16, token_figures, 0)
    figure_mine[...] = figures[...].T[:8, :]
    for place in OTHERS:
        send(figure_mine, figure_all.at[place], figure_send, figure_recv, at(place))
    pltpu.make_async_copy(figure_mine, figure_all.at[OWN], figure_recv).start()

    def gain_part(to):
        return gains.at[:, to // (share // pair), :, pl.ds(pl.multiple_of(to % (share // pair) * pair, pair), pair)]

    @pl.when(me == RELAY)
    def _():
        pltpu.make_async_copy(gains, gains, gain_recv).wait()
        for place in OTHERS:
            to = at(place)
            send(gain_part(to), gain, hand_send.at[place], hand_recv, to)
        pltpu.make_async_copy(gain_part(me), gain, hand_recv).start()

    for i in range(2):
        for place in OTHERS:
            to = at(place)
            send(keys.at[i, :, columns(to, pair)], kraw.at[i, pl.ds(place * tok, tok), :], k_send.at[i], k_recv, to)
        pltpu.make_async_copy(keys.at[i, :, columns(me, pair)], kraw.at[i, pl.ds(OWN * tok, tok), :], k_recv).start()
    for part in range(PARTS):
        rows = pl.ds(part * piece, piece)
        for place in range(16):
            to = at(place)
            block = queries.at[rows, columns(to, 2 * pair)]
            there = qbuf.at[part, place // 4, pl.ds(place % 4 * piece, piece), :]
            if place == OWN:
                pltpu.make_async_copy(block, there, q_recv.at[part, place]).start()
            else:
                send(block, there, q_send, q_recv.at[part, place], to)

    pltpu.make_async_copy(vbuf, vbuf, v_recv).wait()

    def interleave(n, _):
        r = pl.ds(pl.multiple_of(n * 128, 128), 128)
        for h in range(2):
            for i in range(2):
                vcat[r, (2 * h + i) * HD:(2 * h + i + 1) * HD] = vbuf[i, r, h * HD:(h + 1) * HD]
        return 0

    lax.fori_loop(0, length // 128, interleave, 0)
    pltpu.make_async_copy(figure_all, figure_all, figure_recv).wait()

    def upright(place, _):
        figure_of[place] = figure_all[place].T
        return 0

    lax.fori_loop(0, groups, upright, 0)
    pltpu.make_async_copy(gain, gain, hand_recv).wait()
    pltpu.make_async_copy(kraw, kraw, k_recv).wait()

    def norm(a, b, g, inverse, mixed):
        a, b = a.astype(F32), b.astype(F32)
        return (g * a * inverse).astype(BF16), (g * (b * inverse - a * mixed)).astype(BF16)

    def norm_keys(place, _):
        r = pl.ds(pl.multiple_of(place * tok, tok), tok)
        inverse, mixed = figure_of[place, :, 2:3], figure_of[place, :, 3:4]
        for h in range(2):
            cols = slice(h * HD, (h + 1) * HD)
            primal, tangent = norm(kraw[0, r, cols], kraw[1, r, cols], gain[0, :, cols], inverse, mixed)
            kbuf[h, r, :HD] = primal
            kbuf[h, r, HD:] = tangent
        return 0

    lax.fori_loop(0, groups, norm_keys, 0)

    scale = HD ** (-0.5)

    def attend(step, _):
        part, group = step // 4, step % 4
        rows = pl.ds(pl.multiple_of(part * piece, piece), piece)
        for n in range(4):
            block = qbuf.at[part, group, pl.ds(n * piece, piece), :]
            pltpu.make_async_copy(block, block, q_recv.at[part, group * 4 + n]).wait()
        for h in range(2):
            primal, tangent = [], []
            for n in range(4):
                own = figure_of.at[group * 4 + n]
                p, t = norm(
                    qbuf[part, group, n * piece:(n + 1) * piece, pair + h * HD:pair + (h + 1) * HD],
                    qbuf[part, group, n * piece:(n + 1) * piece, h * HD:(h + 1) * HD],
                    gain[1, :, h * HD:(h + 1) * HD], own[rows, 0:1], own[rows, 1:2])
                primal.append(p)
                tangent.append(t)
            primal, tangent = jnp.concatenate(primal, axis=0), jnp.concatenate(tangent, axis=0)
            both_keys = kbuf[h]
            dims = (((1,), (1,)), ((), ()))
            scores = lax.dot_general(primal, both_keys[:, :HD], dims, preferred_element_type=F32)
            scores_tan = lax.dot_general(
                jnp.concatenate([tangent, primal], axis=1), both_keys, dims, preferred_element_type=F32)
            top = jnp.max(scores, axis=1, keepdims=True)
            weights = jnp.exp2((scores - top) * (scale * LOG2E))
            inverse = 1.0 / jnp.sum(weights, axis=1, keepdims=True)
            mean = jnp.sum(weights * scores_tan, axis=1, keepdims=True) * inverse
            low = (weights * inverse).astype(BF16)
            low_tan = (weights * (scores_tan - mean) * (inverse * scale)).astype(BF16)
            both = jnp.dot(low, vcat[:, h * pair:(h + 1) * pair], preferred_element_type=F32)
            rest = jnp.dot(low_tan, vcat[:, h * pair:h * pair + HD], preferred_element_type=F32)
            obuf[step, 0, :, h * HD:(h + 1) * HD] = both[:, :HD].astype(BF16)
            obuf[step, 1, :, h * HD:(h + 1) * HD] = (both[:, HD:] + rest).astype(BF16)
        other, near = group // 2, group % 2
        for n in range(4):
            dx = FAR[n][0] + near * (NEAR[n][0] - FAR[n][0])
            dy = FAR[n][1] + near * (NEAR[n][1] - FAR[n][1])
            owner = ((x + way * dx + 4) % 4) * 4 + ((y + dy) % 2) * 2 + (core + other) % 2
            block = obuf.at[step, :, pl.ds(n * piece, piece), :]
            there = out_hbm.at[:, rows, columns(me, pair)]
            give = functools.partial(send, block, there, o_send, o_recv, owner)
            if n == OWN % 4:
                pl.when(group != OWN // 4)(give)

                @pl.when(group == OWN // 4)
                def _():
                    pltpu.make_async_copy(block, there, o_recv).start()
            else:
                give()
        return 0

    lax.fori_loop(0, PARTS * 4, attend, 0)

    pltpu.make_async_copy(out_hbm, out_hbm, o_recv).wait()
    others = pl.ds(0, length - tok)
    for i in range(2):
        pltpu.make_async_copy(vbuf.at[i, others, :], vbuf.at[i, others, :], v_send.at[i]).wait()
        pltpu.make_async_copy(kraw.at[i, others, :], kraw.at[i, others, :], k_send.at[i]).wait()
    pltpu.make_async_copy(figure_all.at[pl.ds(0, groups - 1)], figure_all.at[pl.ds(0, groups - 1)], figure_send).wait()
    most = pl.ds(0, 4 * piece - piece // 4)
    pltpu.make_async_copy(qbuf.at[:, :, most, :], qbuf.at[:, :, most, :], q_send).wait()
    pltpu.make_async_copy(obuf.at[:, :, most, :], obuf.at[:, :, most, :], o_send).wait()

    @pl.when(me == RELAY)
    def _():
        for i in range(2):
            pltpu.make_async_copy(gains.at[i, pl.ds(0, clips - 1)], gains.at[i, pl.ds(0, clips - 1)], gain_send.at[i]).wait()
        for place in OTHERS:
            pltpu.make_async_copy(gain, gain, hand_send.at[place]).wait()


def hand_out(both, first, second, sems):
    copies = [pltpu.make_async_copy(both.at[i], out, sems.at[i]) for i, out in enumerate((first, second))]
    for copy in copies:
        copy.start()
    for copy in copies:
        copy.wait()


def on_device(query_raw, key_raw, values, query_tan, key_tan, values_tan, query_gain, key_gain):
    tok, width = query_raw.shape
    groups = lax.axis_size("seq")
    clips = lax.axis_size("clip")
    length = tok * groups
    share = query_gain.shape[0]
    pair = 2 * HD
    dma = pltpu.SemaphoreType.DMA
    anywhere = pl.BlockSpec(memory_space=pl.ANY)
    both = pl.pallas_call(
        functools.partial(kernel, clips),
        out_shape=pltpu.VMEM((2, tok, width), BF16),
        in_specs=[anywhere] * 8,
        out_specs=pl.BlockSpec(memory_space=pltpu.VMEM),
        scratch_shapes=[
            pltpu.VMEM((tok, 2 * width), BF16),
            pltpu.VMEM((2, tok, width), BF16),
            pltpu.VMEM((tok, HD), F32),
            pltpu.VMEM((8, tok), F32),
            pltpu.VMEM((groups, 8, tok), F32),
            pltpu.VMEM((groups, tok, 8), F32),
            pltpu.VMEM((2, clips, 1, share), F32),
            pltpu.VMEM((2, 1, pair), F32),
            pltpu.VMEM((2, length, pair), BF16),
            pltpu.VMEM((length, 2 * pair), BF16),
            pltpu.VMEM((2, length, pair), BF16),
            pltpu.VMEM((2, length, pair), BF16),
            pltpu.VMEM((PARTS, 4, length // PARTS // 4, 2 * pair), BF16),
            pltpu.VMEM((PARTS * 4, 2, length // PARTS // 4, pair), BF16),
            dma, dma, dma((2,)), dma, dma((groups,)), dma, dma, dma,
            dma((2,)), dma, dma((2,)), dma, dma, dma((PARTS, groups)), dma, dma,
        ],
        compiler_params=pltpu.CompilerParams(
            collective_id=0, has_side_effects=True, vmem_limit_bytes=56 * 2**20
        ),
        cost_estimate=pl.CostEstimate(flops=13_000_000_000, bytes_accessed=8 * 2**20, transcendentals=8_400_000),
    )(query_raw, key_raw, values, query_tan, key_tan, values_tan,
      query_gain.reshape(1, share), key_gain.reshape(1, share))
    return pl.pallas_call(
        hand_out,
        out_shape=(jax.ShapeDtypeStruct((tok, width), BF16),) * 2,
        in_specs=[pl.BlockSpec(memory_space=pltpu.VMEM)],
        out_specs=(anywhere,) * 2,
        scratch_shapes=[dma((2,))],
    )(pltpu.with_memory_space_constraint(both, pltpu.VMEM))


def solution(mesh):
    tokens = P(("clip", "seq"), None)
    return jax.shard_map(
        on_device, mesh=mesh, in_specs=(tokens,) * 6 + (P("clip"),) * 2, out_specs=(tokens,) * 2, check_vma=False
    )
```

time: 107 us -> 101 us (0.944)
  Pallas kernels: 104 us -> 99.1 us
    pallas_call x1, Pallas kernels: 102 us -> 97.7 us  [on_device(): pl.pallas_call(functools.partial(kernel, clips), out_shape=pltpu.VMEM((2,...]
where the time goes in v3:
time: 101 us; the launch traced here: 99.7 us
  Pallas kernels  99.1 us (98%)
    pallas_call x1, Pallas kernels, on_device(): pl.pallas_call(functools.partial(kernel, clips), out_shape=pltpu.VMEM((2,...  97.7 us

profile of v3, /device:TPU:0, one launch (start us, length us, event | category | flops | bytes accessed | tf_op | source)
XLA Modules:
  0.0 99.7 jit_solution(16716889426735683998)
XLA Ops:
  0.6 97.7 %shard_map.95.both = bf16[2,128,4096]{2,1,0:T(8,128)(2,1)S(1)} custom-call(bf16[128,4096]{1,0:T(8,128)(2,1)} %q_hbm.1, bf16[128,4096]{1,0:T(8,128)(2,1)} %k_hbm.1, bf16[128,4096]{1,0:T(8,128)(2,1)} %v_hbm.1, bf16[128,4096]{1,0:T(8,128)(2,1)} %qt_hbm.1, bf16[128,4096]{1,0:T(8,128)(2,1)} %kt_hbm.1, bf16[128,4096]{1,0:T(8,128)(2,1)} %vt_hbm.1, ...), custom_call_target="tpu_custom_call" | custom-call | flops 12999999488 | bytes 8388608 | tf_op jit(solution)/shard_map/pallas_call | solution.py:278
  98.4 1.3 %shard_map.96 = (bf16[128,4096]{1,0:T(8,128)(2,1)}, bf16[128,4096]{1,0:T(8,128)(2,1)}) custom-call(bf16[2,128,4096]{2,1,0:T(8,128)(2,1)S(1)} %shard_map.95.both), custom_call_target="tpu_custom_call" | custom-call | tf_op jit(solution)/shard_map/pallas_call | solution.py:307

commit v4 on v3

--- a/solution.py
+++ b/solution.py
@@ -15,17 +15,18 @@
 F32 = jnp.float32
 BF16 = jnp.bfloat16
 
-FAR = ((2, 1), (3, 1), (1, 1), (0, 0))
-NEAR = ((0, 1), (2, 0), (3, 0), (1, 0))
+FAR = ((3, 1), (2, 1), (1, 1), (0, 0))
+NEAR = ((0, 1), (3, 0), (2, 0), (1, 0))
 PLACES = tuple((dx, dy, core) for core in range(2) for chips in (FAR, NEAR) for dx, dy in chips)
 OWN = PLACES.index((0, 0, 0))
 OTHERS = tuple(p for p in range(16) if p != OWN)
 PARTS = 2
+CHUNKS = 4
 RELAY = 0
 
 
 def kernel(clips, q_hbm, k_hbm, v_hbm, qt_hbm, kt_hbm, vt_hbm, gq_hbm, gk_hbm, out_hbm,
-           queries, keys, figures, figure_mine, figure_all, figure_of, gains, gain,
+           queries, keys, figures, figure_mine, figure_all, figure_of, gains, gain, handed_out,
            vbuf, vcat, kraw, kbuf, qbuf, obuf,
            load_k, load_q, gain_send, gain_recv, hand_send, hand_recv, figure_send, figure_recv,
            v_send, v_recv, k_send, k_recv, q_send, q_recv, o_send, o_recv):
@@ -44,12 +45,37 @@
         dx, dy, other = PLACES[place]
         return ((x + way * dx + 4) % 4) * 4 + ((y + dy) % 2) * 2 + (core + other) % 2
 
+    def visit(turn, act):
+        group = (turn + 1 - core) % 4
+        other, near = group // 2, group % 2
+        for n in range(4):
+            dx = FAR[n][0] + near * (NEAR[n][0] - FAR[n][0])
+            dy = FAR[n][1] + near * (NEAR[n][1] - FAR[n][1])
+            to = ((x + way * dx + 4) % 4) * 4 + ((y + dy) % 2) * 2 + (core + other) % 2
+            act_here = functools.partial(act, group, n, to)
+            if n == OWN % 4:
+                pl.when(group != OWN // 4)(act_here)
+            else:
+                act_here()
+
+    def rows_of(group, n):
+        return pl.ds(pl.multiple_of((group * 4 + n) * tok, tok), tok)
+
     def columns(index, size):
         return pl.ds(pl.multiple_of(index * size, size), size)
 
     def send(src, dst, send_sem, recv_sem, to):
         pltpu.make_async_remote_copy(
             src_ref=src, dst_ref=dst, send_sem=send_sem, recv_sem=recv_sem, device_id=(clip, to), device_id_type=MESH).start()
+
+    barrier = pltpu.get_barrier_semaphore()
+    for place in OTHERS:
+        pl.semaphore_signal(barrier, inc=1, device_id=(clip, at(place)), device_id_type=MESH)
+
+    @pl.when(me == RELAY)
+    def _():
+        for step in range(1, clips):
+            pl.semaphore_signal(barrier, inc=1, device_id=((clip + step) % clips, me), device_id_type=MESH)
 
     for i, src in enumerate((k_hbm, kt_hbm)):
         pltpu.make_async_copy(src, keys.at[i], load_k).start()
@@ -58,15 +84,6 @@
             pltpu.make_async_copy(
                 src.at[:, n * pair:(n + 1) * pair], queries.at[:, (2 * n + i) * pair:(2 * n + i + 1) * pair], load_q).start()
 
-    barrier = pltpu.get_barrier_semaphore()
-    for place in OTHERS:
-        pl.semaphore_signal(barrier, inc=1, device_id=(clip, at(place)), device_id_type=MESH)
-
-    @pl.when(me == RELAY)
-    def _():
-        for step in range(1, clips):
-            pl.semaphore_signal(barrier, inc=1, device_id=((clip + step) % clips, me), device_id_type=MESH)
-
     @pl.when(me != RELAY)
     def _():
         pl.semaphore_wait(barrier, len(OTHERS))
@@ -77,14 +94,16 @@
         for i, src in enumerate((gk_hbm, gq_hbm)):
             for step in range(1, clips):
                 pltpu.make_async_remote_copy(
-                    src_ref=src, dst_ref=gains.at[i, clip], send_sem=gain_send.at[i], recv_sem=gain_recv,
+                    src_ref=src, dst_ref=gains.at[i, clip], send_sem=gain_send, recv_sem=gain_recv,
                     device_id=((clip + step) % clips, me), device_id_type=MESH).start()
             pltpu.make_async_copy(src, gains.at[i, clip], gain_recv).start()
 
     for i, src in enumerate((v_hbm, vt_hbm)):
-        for place in OTHERS:
-            to = at(place)
-            send(src.at[:, columns(to, pair)], vbuf.at[i, pl.ds(place * tok, tok), :], v_send.at[i], v_recv, to)
+        def give(group, n, to, i=i, src=src):
+            send(src.at[:, columns(to, pair)], vbuf.at[i, rows_of(group, n), :], v_send, v_recv, to)
+
+        for turn in range(4):
+            visit(turn, give)
         pltpu.make_async_copy(src.at[:, columns(me, pair)], vbuf.at[i, pl.ds(OWN * tok, tok), :], v_recv).start()
 
     pltpu.make_async_copy(keys, keys, load_k).wait()
@@ -118,7 +137,7 @@
         return 0
 
     lax.fori_loop(0, tok // 16, token_figures, 0)
-    figure_mine[...] = figures[...].T[:8, :]
+    figure_mine[...] = figures[...].T[:4, :]
     for place in OTHERS:
         send(figure_mine, figure_all.at[place], figure_send, figure_recv, at(place))
     pltpu.make_async_copy(figure_mine, figure_all.at[OWN], figure_recv).start()
@@ -131,24 +150,28 @@
         pltpu.make_async_copy(gains, gains, gain_recv).wait()
         for place in OTHERS:
             to = at(place)
-            send(gain_part(to), gain, hand_send.at[place], hand_recv, to)
+            send(gain_part(to), gain, hand_send, hand_recv, to)
         pltpu.make_async_copy(gain_part(me), gain, hand_recv).start()
 
     for i in range(2):
-        for place in OTHERS:
-            to = at(place)
-            send(keys.at[i, :, columns(to, pair)], kraw.at[i, pl.ds(place * tok, tok), :], k_send.at[i], k_recv, to)
+        def give(group, n, to, i=i):
+            send(keys.at[i, :, columns(to, pair)], kraw.at[i, rows_of(group, n), :], k_send, k_recv, to)
+
+        for turn in range(4):
+            visit(turn, give)
         pltpu.make_async_copy(keys.at[i, :, columns(me, pair)], kraw.at[i, pl.ds(OWN * tok, tok), :], k_recv).start()
     for part in range(PARTS):
         rows = pl.ds(part * piece, piece)
-        for place in range(16):
-            to = at(place)
-            block = queries.at[rows, columns(to, 2 * pair)]
-            there = qbuf.at[part, place // 4, pl.ds(place % 4 * piece, piece), :]
-            if place == OWN:
-                pltpu.make_async_copy(block, there, q_recv.at[part, place]).start()
-            else:
-                send(block, there, q_send, q_recv.at[part, place], to)
+
+        def give(group, n, to, part=part, rows=rows):
+            send(queries.at[rows, columns(to, 2 * pair)], qbuf.at[part, group, pl.ds(n * piece, piece), :],
+                 q_send, q_recv.at[part, group], to)
+
+        for turn in range(4):
+            visit(turn, give)
+        pltpu.make_async_copy(
+            queries.at[rows, columns(me, 2 * pair)], qbuf.at[part, OWN // 4, pl.ds(OWN % 4 * piece, piece), :],
+            q_recv.at[part, OWN // 4]).start()
 
     pltpu.make_async_copy(vbuf, vbuf, v_recv).wait()
 
@@ -189,11 +212,11 @@
     scale = HD ** (-0.5)
 
     def attend(step, _):
-        part, group = step // 4, step % 4
+        part, turn = step // 4, step % 4
+        group = (turn + 1 - core) % 4
         rows = pl.ds(pl.multiple_of(part * piece, piece), piece)
-        for n in range(4):
-            block = qbuf.at[part, group, pl.ds(n * piece, piece), :]
-            pltpu.make_async_copy(block, block, q_recv.at[part, group * 4 + n]).wait()
+        block = qbuf.at[part, group]
+        pltpu.make_async_copy(block, block, q_recv.at[part, group]).wait()
         for h in range(2):
             primal, tangent = [], []
             for n in range(4):
@@ -220,31 +243,25 @@
             rest = jnp.dot(low_tan, vcat[:, h * pair:h * pair + HD], preferred_element_type=F32)
             obuf[step, 0, :, h * HD:(h + 1) * HD] = both[:, :HD].astype(BF16)
             obuf[step, 1, :, h * HD:(h + 1) * HD] = (both[:, HD:] + rest).astype(BF16)
-        other, near = group // 2, group % 2
-        for n in range(4):
-            dx = FAR[n][0] + near * (NEAR[n][0] - FAR[n][0])
-            dy = FAR[n][1] + near * (NEAR[n][1] - FAR[n][1])
-            owner = ((x + way * dx + 4) % 4) * 4 + ((y + dy) % 2) * 2 + (core + other) % 2
-            block = obuf.at[step, :, pl.ds(n * piece, piece), :]
-            there = out_hbm.at[:, rows, columns(me, pair)]
-            give = functools.partial(send, block, there, o_send, o_recv, owner)
-            if n == OWN % 4:
-                pl.when(group != OWN // 4)(give)
-
-                @pl.when(group == OWN // 4)
-                def _():
-                    pltpu.make_async_copy(block, there, o_recv).start()
-            else:
-                give()
+
+        def give(group, n, to):
+            send(obuf.at[step, :, pl.ds(n * piece, piece), :], out_hbm.at[:, rows, columns(me, pair)], o_send, o_recv, to)
+
+        visit(turn, give)
+
+        @pl.when(group == OWN // 4)
+        def _():
+            pltpu.make_async_copy(
+                obuf.at[step, :, pl.ds(OWN % 4 * piece, piece), :], out_hbm.at[:, rows, columns(me, pair)], o_recv).start()
+
         return 0
 
     lax.fori_loop(0, PARTS * 4, attend, 0)
 
     pltpu.make_async_copy(out_hbm, out_hbm, o_recv).wait()
     others = pl.ds(0, length - tok)
-    for i in range(2):
-        pltpu.make_async_copy(vbuf.at[i, others, :], vbuf.at[i, others, :], v_send.at[i]).wait()
-        pltpu.make_async_copy(kraw.at[i, others, :], kraw.at[i, others, :], k_send.at[i]).wait()
+    pltpu.make_async_copy(vbuf.at[:, others, :], vbuf.at[:, others, :], v_send).wait()
+    pltpu.make_async_copy(kraw.at[:, others, :], kraw.at[:, others, :], k_send).wait()
     pltpu.make_async_copy(figure_all.at[pl.ds(0, groups - 1)], figure_all.at[pl.ds(0, groups - 1)], figure_send).wait()
     most = pl.ds(0, 4 * piece - piece // 4)
     pltpu.make_async_copy(qbuf.at[:, :, most, :], qbuf.at[:, :, most, :], q_send).wait()
@@ -252,14 +269,17 @@
 
     @pl.when(me == RELAY)
     def _():
-        for i in range(2):
-            pltpu.make_async_copy(gains.at[i, pl.ds(0, clips - 1)], gains.at[i, pl.ds(0, clips - 1)], gain_send.at[i]).wait()
-        for place in OTHERS:
-            pltpu.make_async_copy(gain, gain, hand_send.at[place]).wait()
+        met = gains.at[:, pl.ds(0, clips - 1)]
+        pltpu.make_async_copy(met, met, gain_send).wait()
+        handed = handed_out.at[pl.ds(0, groups - 1)]
+        pltpu.make_async_copy(handed, handed, hand_send).wait()
 
 
 def hand_out(both, first, second, sems):
-    copies = [pltpu.make_async_copy(both.at[i], out, sems.at[i]) for i, out in enumerate((first, second))]
+    rows = both.shape[1] // CHUNKS
+    copies = [
+        pltpu.make_async_copy(both.at[i, pl.ds(n * rows, rows), :], out.at[pl.ds(n * rows, rows), :], sems.at[i, n])
+        for n in range(CHUNKS) for i, out in enumerate((first, second))]
     for copy in copies:
         copy.start()
     for copy in copies:
@@ -284,19 +304,20 @@
             pltpu.VMEM((tok, 2 * width), BF16),
             pltpu.VMEM((2, tok, width), BF16),
             pltpu.VMEM((tok, HD), F32),
-            pltpu.VMEM((8, tok), F32),
-            pltpu.VMEM((groups, 8, tok), F32),
-            pltpu.VMEM((groups, tok, 8), F32),
+            pltpu.VMEM((4, tok), F32),
+            pltpu.VMEM((groups, 4, tok), F32),
+            pltpu.VMEM((groups, tok, 4), F32),
             pltpu.VMEM((2, clips, 1, share), F32),
             pltpu.VMEM((2, 1, pair), F32),
+            pltpu.VMEM((groups, 2, 1, pair), F32),
             pltpu.VMEM((2, length, pair), BF16),
             pltpu.VMEM((length, 2 * pair), BF16),
             pltpu.VMEM((2, length, pair), BF16),
             pltpu.VMEM((2, length, pair), BF16),
             pltpu.VMEM((PARTS, 4, length // PARTS // 4, 2 * pair), BF16),
             pltpu.VMEM((PARTS * 4, 2, length // PARTS // 4, pair), BF16),
-            dma, dma, dma((2,)), dma, dma((groups,)), dma, dma, dma,
-            dma((2,)), dma, dma((2,)), dma, dma, dma((PARTS, groups)), dma, dma,
+            dma, dma, dma, dma, dma, dma, dma, dma,
+            dma, dma, dma, dma, dma, dma((PARTS, 4)), dma, dma,
         ],
         compiler_params=pltpu.CompilerParams(
             collective_id=0, has_side_effects=True, vmem_limit_bytes=56 * 2**20
@@ -309,7 +330,7 @@
         out_shape=(jax.ShapeDtypeStruct((tok, width), BF16),) * 2,
         in_specs=[pl.BlockSpec(memory_space=pltpu.VMEM)],
         out_specs=(anywhere,) * 2,
-        scratch_shapes=[dma((2,))],
+        scratch_shapes=[dma((2, CHUNKS))],
     )(pltpu.with_memory_space_constraint(both, pltpu.VMEM))
 
 

time: 101 us -> 99.5 us (0.985); the launches traced: 99.7 us -> 99.3 us
  no operation moved by 1% of the time
where the time goes in v4:
time: 99.5 us; the launch traced here: 99.3 us
  Pallas kernels  98.7 us (99%)
    pallas_call x1, Pallas kernels, on_device(): pl.pallas_call(functools.partial(kernel, clips), out_shape=pltpu.VMEM((2,...  97.3 us

profile of v4, /device:TPU:0, one launch (start us, length us, event | category | flops | bytes accessed | tf_op | source)
XLA Modules:
  0.0 99.3 jit_solution(10822142768323971040)
XLA Ops:
  0.6 97.3 %shard_map.95.both = bf16[2,128,4096]{2,1,0:T(8,128)(2,1)S(1)} custom-call(bf16[128,4096]{1,0:T(8,128)(2,1)} %q_hbm.1, bf16[128,4096]{1,0:T(8,128)(2,1)} %k_hbm.1, bf16[128,4096]{1,0:T(8,128)(2,1)} %v_hbm.1, bf16[128,4096]{1,0:T(8,128)(2,1)} %qt_hbm.1, bf16[128,4096]{1,0:T(8,128)(2,1)} %kt_hbm.1, bf16[128,4096]{1,0:T(8,128)(2,1)} %vt_hbm.1, ...), custom_call_target="tpu_custom_call" | custom-call | flops 12999999488 | bytes 8388608 | tf_op jit(solution)/shard_map/pallas_call | solution.py:298
  98.0 1.4 %shard_map.96 = (bf16[128,4096]{1,0:T(8,128)(2,1)}, bf16[128,4096]{1,0:T(8,128)(2,1)}) custom-call(bf16[2,128,4096]{2,1,0:T(8,128)(2,1)S(1)} %shard_map.95.both), custom_call_target="tpu_custom_call" | custom-call | tf_op jit(solution)/shard_map/pallas_call | solution.py:328

commit v5 on v4

--- a/solution.py
+++ b/solution.py
@@ -79,10 +79,8 @@
 
     for i, src in enumerate((k_hbm, kt_hbm)):
         pltpu.make_async_copy(src, keys.at[i], load_k).start()
-    for n in range(groups):
-        for i, src in enumerate((qt_hbm, q_hbm)):
-            pltpu.make_async_copy(
-                src.at[:, n * pair:(n + 1) * pair], queries.at[:, (2 * n + i) * pair:(2 * n + i + 1) * pair], load_q).start()
+    for i, src in enumerate((q_hbm, qt_hbm)):
+        pltpu.make_async_copy(src, queries.at[i], load_q).start()
 
     @pl.when(me != RELAY)
     def _():
@@ -121,14 +119,10 @@
             inverse = 1.0 / jnp.sqrt(jnp.sum(square, axis=1, keepdims=True) / width + EPS)
             return inverse, jnp.sum(cross, axis=1, keepdims=True) / width * (inverse * inverse * inverse)
 
-        def query_part(i):
-            def part(h):
-                start = (2 * (h // 2) + i) * pair + h % 2 * HD
-                return queries[r, start:start + HD]
-            return part
-
-        found = pair_of(query_part(1), query_part(0)) + pair_of(
-            lambda h: keys[0, r, h * HD:(h + 1) * HD], lambda h: keys[1, r, h * HD:(h + 1) * HD])
+        def head_of(array, i):
+            return lambda h: array[i, r, h * HD:(h + 1) * HD]
+
+        found = pair_of(head_of(queries, 0), head_of(queries, 1)) + pair_of(head_of(keys, 0), head_of(keys, 1))
         lane = lax.broadcasted_iota(jnp.int32, (16, HD), 1)
         row = jnp.zeros((16, HD), F32)
         for i, value in enumerate(found):
@@ -164,13 +158,13 @@
         rows = pl.ds(part * piece, piece)
 
         def give(group, n, to, part=part, rows=rows):
-            send(queries.at[rows, columns(to, 2 * pair)], qbuf.at[part, group, pl.ds(n * piece, piece), :],
+            send(queries.at[:, rows, columns(to, pair)], qbuf.at[part, group, :, pl.ds(n * piece, piece), :],
                  q_send, q_recv.at[part, group], to)
 
         for turn in range(4):
             visit(turn, give)
         pltpu.make_async_copy(
-            queries.at[rows, columns(me, 2 * pair)], qbuf.at[part, OWN // 4, pl.ds(OWN % 4 * piece, piece), :],
+            queries.at[:, rows, columns(me, pair)], qbuf.at[part, OWN // 4, :, pl.ds(OWN % 4 * piece, piece), :],
             q_recv.at[part, OWN // 4]).start()
 
     pltpu.make_async_copy(vbuf, vbuf, v_recv).wait()
@@ -222,8 +216,8 @@
             for n in range(4):
                 own = figure_of.at[group * 4 + n]
                 p, t = norm(
-                    qbuf[part, group, n * piece:(n + 1) * piece, pair + h * HD:pair + (h + 1) * HD],
-                    qbuf[part, group, n * piece:(n + 1) * piece, h * HD:(h + 1) * HD],
+                    qbuf[part, group, 0, n * piece:(n + 1) * piece, h * HD:(h + 1) * HD],
+                    qbuf[part, group, 1, n * piece:(n + 1) * piece, h * HD:(h + 1) * HD],
                     gain[1, :, h * HD:(h + 1) * HD], own[rows, 0:1], own[rows, 1:2])
                 primal.append(p)
                 tangent.append(t)
@@ -264,7 +258,7 @@
     pltpu.make_async_copy(kraw.at[:, others, :], kraw.at[:, others, :], k_send).wait()
     pltpu.make_async_copy(figure_all.at[pl.ds(0, groups - 1)], figure_all.at[pl.ds(0, groups - 1)], figure_send).wait()
     most = pl.ds(0, 4 * piece - piece // 4)
-    pltpu.make_async_copy(qbuf.at[:, :, most, :], qbuf.at[:, :, most, :], q_send).wait()
+    pltpu.make_async_copy(qbuf.at[:, :, :, most, :], qbuf.at[:, :, :, most, :], q_send).wait()
     pltpu.make_async_copy(obuf.at[:, :, most, :], obuf.at[:, :, most, :], o_send).wait()
 
     @pl.when(me == RELAY)
@@ -301,7 +295,7 @@
         in_specs=[anywhere] * 8,
         out_specs=pl.BlockSpec(memory_space=pltpu.VMEM),
         scratch_shapes=[
-            pltpu.VMEM((tok, 2 * width), BF16),
+            pltpu.VMEM((2, tok, width), BF16),
             pltpu.VMEM((2, tok, width), BF16),
             pltpu.VMEM((tok, HD), F32),
             pltpu.VMEM((4, tok), F32),
@@ -314,7 +308,7 @@
             pltpu.VMEM((length, 2 * pair), BF16),
             pltpu.VMEM((2, length, pair), BF16),
             pltpu.VMEM((2, length, pair), BF16),
-            pltpu.VMEM((PARTS, 4, length // PARTS // 4, 2 * pair), BF16),
+            pltpu.VMEM((PARTS, 4, 2, length // PARTS // 4, pair), BF16),
             pltpu.VMEM((PARTS * 4, 2, length // PARTS // 4, pair), BF16),
             dma, dma, dma, dma, dma, dma, dma, dma,
             dma, dma, dma, dma, dma, dma((PARTS, 4)), dma, dma,

time: 99.5 us -> 99.5 us (level)
  no operation moved by 1% of the time
where the time goes in v5:
time: 99.5 us; the launch traced here: 99.3 us
  Pallas kernels  98.7 us (99%)
    pallas_call x1, Pallas kernels, on_device(): pl.pallas_call(functools.partial(kernel, clips), out_shape=pltpu.VMEM((2,...  97.3 us

profile of v5, /device:TPU:0, one launch (start us, length us, event | category | flops | bytes accessed | tf_op | source)
XLA Modules:
  0.0 99.3 jit_solution(15295670025227851250)
XLA Ops:
  0.6 97.3 %shard_map.95.both = bf16[2,128,4096]{2,1,0:T(8,128)(2,1)S(1)} custom-call(bf16[128,4096]{1,0:T(8,128)(2,1)} %q_hbm.1, bf16[128,4096]{1,0:T(8,128)(2,1)} %k_hbm.1, bf16[128,4096]{1,0:T(8,128)(2,1)} %v_hbm.1, bf16[128,4096]{1,0:T(8,128)(2,1)} %qt_hbm.1, bf16[128,4096]{1,0:T(8,128)(2,1)} %kt_hbm.1, bf16[128,4096]{1,0:T(8,128)(2,1)} %vt_hbm.1, ...), custom_call_target="tpu_custom_call" | custom-call | flops 12999999488 | bytes 8388608 | tf_op jit(solution)/shard_map/pallas_call | solution.py:292
  98.0 1.4 %shard_map.96 = (bf16[128,4096]{1,0:T(8,128)(2,1)}, bf16[128,4096]{1,0:T(8,128)(2,1)}) custom-call(bf16[2,128,4096]{2,1,0:T(8,128)(2,1)S(1)} %shard_map.95.both), custom_call_target="tpu_custom_call" | custom-call | tf_op jit(solution)/shard_map/pallas_call | solution.py:322

commit v6 on v5

--- a/solution.py
+++ b/solution.py
@@ -77,11 +77,6 @@
         for step in range(1, clips):
             pl.semaphore_signal(barrier, inc=1, device_id=((clip + step) % clips, me), device_id_type=MESH)
 
-    for i, src in enumerate((k_hbm, kt_hbm)):
-        pltpu.make_async_copy(src, keys.at[i], load_k).start()
-    for i, src in enumerate((q_hbm, qt_hbm)):
-        pltpu.make_async_copy(src, queries.at[i], load_q).start()
-
     @pl.when(me != RELAY)
     def _():
         pl.semaphore_wait(barrier, len(OTHERS))
@@ -103,6 +98,11 @@
         for turn in range(4):
             visit(turn, give)
         pltpu.make_async_copy(src.at[:, columns(me, pair)], vbuf.at[i, pl.ds(OWN * tok, tok), :], v_recv).start()
+
+    for i, src in enumerate((k_hbm, kt_hbm)):
+        pltpu.make_async_copy(src, keys.at[i], load_k).start()
+    for i, src in enumerate((q_hbm, qt_hbm)):
+        pltpu.make_async_copy(src, queries.at[i], load_q).start()
 
     pltpu.make_async_copy(keys, keys, load_k).wait()
     pltpu.make_async_copy(queries, queries, load_q).wait()

time: 99.5 us -> 99.5 us (level)
  no operation moved by 1% of the time
where the time goes in v6:
time: 99.5 us; the launch traced here: 99.3 us
  Pallas kernels  98.7 us (99%)
    pallas_call x1, Pallas kernels, on_device(): pl.pallas_call(functools.partial(kernel, clips), out_shape=pltpu.VMEM((2,...  97.3 us

profile of v6, /device:TPU:0, one launch (start us, length us, event | category | flops | bytes accessed | tf_op | source)
XLA Modules:
  0.0 99.3 jit_solution(13892515518417093544)
XLA Ops:
  0.6 97.3 %shard_map.95.both = bf16[2,128,4096]{2,1,0:T(8,128)(2,1)S(1)} custom-call(bf16[128,4096]{1,0:T(8,128)(2,1)} %q_hbm.1, bf16[128,4096]{1,0:T(8,128)(2,1)} %k_hbm.1, bf16[128,4096]{1,0:T(8,128)(2,1)} %v_hbm.1, bf16[128,4096]{1,0:T(8,128)(2,1)} %qt_hbm.1, bf16[128,4096]{1,0:T(8,128)(2,1)} %kt_hbm.1, bf16[128,4096]{1,0:T(8,128)(2,1)} %vt_hbm.1, ...), custom_call_target="tpu_custom_call" | custom-call | flops 12999999488 | bytes 8388608 | tf_op jit(solution)/shard_map/pallas_call | solution.py:292
  98.0 1.4 %shard_map.96 = (bf16[128,4096]{1,0:T(8,128)(2,1)}, bf16[128,4096]{1,0:T(8,128)(2,1)}) custom-call(bf16[2,128,4096]{2,1,0:T(8,128)(2,1)S(1)} %shard_map.95.both), custom_call_target="tpu_custom_call" | custom-call | tf_op jit(solution)/shard_map/pallas_call | solution.py:322

commit v7 on v6

--- a/solution.py
+++ b/solution.py
@@ -21,7 +21,7 @@
 OWN = PLACES.index((0, 0, 0))
 OTHERS = tuple(p for p in range(16) if p != OWN)
 PARTS = 2
-CHUNKS = 4
+CHUNKS = 1
 RELAY = 0
 
 

time: 99.5 us -> 99.4 us (level)
  no operation moved by 1% of the time
where the time goes in v7:
time: 99.4 us; the launch traced here: 99.3 us
  Pallas kernels  98.7 us (99%)
    pallas_call x1, Pallas kernels, on_device(): pl.pallas_call(functools.partial(kernel, clips), out_shape=pltpu.VMEM((2,...  97.3 us

profile of v7, /device:TPU:0, one launch (start us, length us, event | category | flops | bytes accessed | tf_op | source)
XLA Modules:
  0.0 99.3 jit_solution(980886737680534590)
XLA Ops:
  0.6 97.3 %shard_map.95.both = bf16[2,128,4096]{2,1,0:T(8,128)(2,1)S(1)} custom-call(bf16[128,4096]{1,0:T(8,128)(2,1)} %q_hbm.1, bf16[128,4096]{1,0:T(8,128)(2,1)} %k_hbm.1, bf16[128,4096]{1,0:T(8,128)(2,1)} %v_hbm.1, bf16[128,4096]{1,0:T(8,128)(2,1)} %qt_hbm.1, bf16[128,4096]{1,0:T(8,128)(2,1)} %kt_hbm.1, bf16[128,4096]{1,0:T(8,128)(2,1)} %vt_hbm.1, ...), custom_call_target="tpu_custom_call" | custom-call | flops 12999999488 | bytes 8388608 | tf_op jit(solution)/shard_map/pallas_call | solution.py:292
  98.0 1.3 %shard_map.96 = (bf16[128,4096]{1,0:T(8,128)(2,1)}, bf16[128,4096]{1,0:T(8,128)(2,1)}) custom-call(bf16[2,128,4096]{2,1,0:T(8,128)(2,1)S(1)} %shard_map.95.both), custom_call_target="tpu_custom_call" | custom-call | tf_op jit(solution)/shard_map/pallas_call | solution.py:322
